TPU v7x, 512 devices: a whole 4x8x8 slice. The times are simulated.
512 devices in a mesh: row: 32 (over z, x_hi, core), col: 16 (over x_lo, y).
Axes of the slice: x: 4 (x_hi: 2, x_lo: 2; x = x_hi * 2 + x_lo), y: 8, z: 8, core: 2. Of those that a mesh axis runs over, the one named last changes fastest.
Arguments:
- trunk_in: bfloat16 [1536, 32768], P('col', 'row'), may hold values from -24 to 24
- conv_weight: bfloat16 [5, 1536, 1536], P(None, 'col'), may hold values from -0.0625 to 0.0625
- conv_bias: float32 [1536], P('col'), may hold values from -3 to 3
- norm_gain: float32 [1536], replicated, may hold values from 0.1 to 1.9
- pair_proj: bfloat16 [64, 1536], replicated, may hold values from -0.15625 to 0.15625
- pair_in: bfloat16 [2048, 512, 128], P('row', 'col'), may hold values from -6 to 6
- opm_weight: bfloat16 [1024, 128], replicated, may hold values from -0.1875 to 0.1875
- pair_bias: float32 [128], replicated, may hold values from -3 to 3
Outputs:
- trunk_out: bfloat16 [1536, 32768], P('col', 'row')
- pair_out: bfloat16 [2048, 512, 128], P('row', 'col')
All inputs are finite; a program needn't handle non-finite values.
Results may differ from a plain program's by a relative error of at most 0.012.
Values may be sent and summed in bfloat16 or wider, within the bound.
A program may use at most 64 MiB of HBM per device.

v0:
```python
import jax
import jax.numpy as jnp
from jax import lax
from jax.sharding import PartitionSpec as P

TRUNK_CHANNELS = 1536
DILATION_STEP = 8
POOL = 16
OPM = 32
WINDOWS = 4


EPSILON = 1e-05


def with_halo(cells, sides, width):
    for axis, dim in sides:
        count = lax.axis_size(axis)
        ends = count - 1
        head = lax.slice_in_dim(cells, 0, width, axis=dim)
        tail = lax.slice_in_dim(cells, cells.shape[dim] - width, cells.shape[dim], axis=dim)
        cells = jnp.concatenate(
            [
                lax.ppermute(tail, axis, [(i, (i + 1) % count) for i in range(ends)]),
                cells,
                lax.ppermute(head, axis, [((i + 1) % count, i) for i in range(ends)]),
            ],
            axis=dim,
        )
    return cells


def partner_2(block, axis, bit):
    count = lax.axis_size(axis)
    route = []
    for low in range(count):
        high = low | 1 << bit
        if high != low and high < count:
            route += [(low, high), (high, low)]
    return lax.ppermute(block, axis, route)


def per_device(
    trunk_in, conv_weight, conv_bias, norm_gain, pair_proj, pair_in, opm_weight, pair_bias
):
    local_channels = trunk_in.shape[0]
    token_positions = trunk_in.shape[1]
    kernel = conv_weight.shape[0]
    border_width = 2 * DILATION_STEP
    per_window = lax.axis_size("row") // WINDOWS
    row_index = lax.axis_index("row")
    col_index = lax.axis_index("col")
    in_window = row_index % per_window
    source = trunk_in.astype(jnp.float32)
    zero_sum = jnp.zeros((local_channels, token_positions), jnp.float32)
    gathered = lax.all_gather(trunk_in, "col", axis=0, tiled=True)
    padded_trunk = with_halo(gathered, (("row", 1),), border_width)
    values = padded_trunk.astype(jnp.float32)
    scale = lax.rsqrt(jnp.mean(values * values, axis=0, keepdims=True) + EPSILON)
    gelu_output = jax.nn.gelu(values * norm_gain[:, None] * scale).astype(jnp.bfloat16)
    conv_sum = zero_sum
    for tap_offset in range(kernel):
        conv_sum = conv_sum + jnp.dot(
            conv_weight[tap_offset],
            gelu_output[
                :, tap_offset * DILATION_STEP : tap_offset * DILATION_STEP + token_positions
            ],
            preferred_element_type=jnp.float32,
        )
    trunk_out = (source + conv_sum + conv_bias[:, None]).astype(jnp.bfloat16)
    pooled = (
        trunk_out.astype(jnp.float32)
        .reshape(local_channels, token_positions // POOL, POOL)
        .mean(axis=2)
        .astype(jnp.bfloat16)
    )
    own_proj = lax.dynamic_slice_in_dim(pair_proj, col_index * local_channels, local_channels, 1)
    pooled_f = pooled.astype(jnp.float32)
    partial_proj = lax.dot_general(
        pooled, own_proj, (((0,), (1,)), ((), ())), preferred_element_type=jnp.float32
    )
    projected, sums = lax.psum((partial_proj, jnp.sum(pooled_f * pooled_f, axis=0)), "col")
    sides = (projected * lax.rsqrt(sums / TRUNK_CHANNELS + EPSILON)[:, None]).astype(jnp.bfloat16)
    row_side = sides[:, :OPM]
    collected = sides[:, OPM:]
    col_block = pair_in.shape[1]
    pooled_rows = row_side.shape[0]
    for bit_num in range(per_window.bit_length() - 1):
        partner = partner_2(collected, "row", bit_num)
        upper_half = in_window // 2**bit_num % 2 == 1
        collected = jnp.where(
            upper_half,
            jnp.concatenate([partner, collected], axis=0),
            jnp.concatenate([collected, partner], axis=0),
        )
    own_cols = lax.dynamic_slice_in_dim(collected, col_index * col_block, col_block, 0)
    outer = (
        row_side.astype(jnp.float32)[:, None, :, None]
        * own_cols.astype(jnp.float32)[None, :, None, :]
    ).astype(jnp.bfloat16)
    outer = outer.reshape(pooled_rows * col_block, OPM * OPM)
    update = jnp.dot(outer, opm_weight, preferred_element_type=jnp.float32).reshape(pair_in.shape)
    pair_out = (pair_in.astype(jnp.float32) + update + pair_bias).astype(jnp.bfloat16)
    return (trunk_out, pair_out)


def solution(mesh):
    return jax.shard_map(
        per_device,
        mesh=mesh,
        in_specs=(
            P("col", "row"),
            P(None, "col", None),
            P("col"),
            P(),
            P(),
            P("row", "col", None),
            P(),
            P(),
        ),
        out_specs=(P("col", "row"), P("row", "col", None)),
        check_vma=False,
    )
```

profile of v0, /device:TPU:1, one launch (start us, length us, event | category | flops | bytes accessed | tf_op | source)
XLA Modules:
  0.0 213.9 jit_solution(7731478625536114508)
XLA Ops:
  7.2 0.0 copy-start
  7.2 0.0 all-gather.2.cloned.1.call-start
  7.2 0.7 all-gather.2.cloned.1.call-update
  7.9 75.2 %all-gather.2.cloned.1.call-done = bf16[1536,1024]{1,0:T(8,128)(2,1)} async-done(((bf16[96,1024]{1,0:T(8,128)(2,1)}), bf16[1536,1024]{1,0:T(8,128)(2,1)}) %all-gather.2.cloned.1.call-update) | async-done | bytes 3145744 | tf_op jit(solution)/shard_map/all_gather | solution.py:56
  83.2 1.3 fusion.69
  84.5 14.6 %collective-permute-start = (bf16[1536,16]{1,0:T(8,128)(2,1)S(1)}, bf16[1536,16]{1,0:T(8,128)(2,1)S(1)}, u32[]{:S(2)}, u32[]{:S(2)}) collective-permute-start(bf16[1536,16]{1,0:T(8,128)(2,1)S(1)} %get-tuple-element.5), channel_id=1, source_target_pairs={{0,16},{16,32},{32,48},{48,64},{64,80},{80,96},{96,112},{112,128},... | collective-permute-start | bytes 147464 | tf_op jit(solution)/shard_map/ppermute | solution.py:24
  99.0 1.9 collective-permute-start.1
  101.0 2.8 %collective-permute-done = bf16[1536,16]{1,0:T(8,128)(2,1)S(1)} collective-permute-done((bf16[1536,16]{1,0:T(8,128)(2,1)S(1)}, bf16[1536,16]{1,0:T(8,128)(2,1)S(1)}, u32[]{:S(2)}, u32[]{:S(2)}) %collective-permute-start) | collective-permute-done | bytes 49184 | tf_op jit(solution)/shard_map/ppermute | solution.py:24
  103.7 5.9 %collective-permute-done.1 = bf16[1536,16]{1,0:T(8,128)(2,1)S(1)} collective-permute-done((bf16[1536,16]{1,0:T(8,128)(2,1)S(1)}, bf16[1536,16]{1,0:T(8,128)(2,1)S(1)}, u32[]{:S(2)}, u32[]{:S(2)}) %collective-permute-start.1) | collective-permute-done | bytes 49184 | tf_op jit(solution)/shard_map/ppermute | solution.py:26
  109.6 7.5 %concatenate.21 = bf16[1536,1056]{1,0:T(8,128)(2,1)} concatenate(bf16[1536,16]{1,0:T(8,128)(2,1)S(1)} %collective-permute-done, bf16[1536,1024]{1,0:T(8,128)(2,1)} %all-gather.2.cloned.1.call-done, bf16[1536,16]{1,0:T(8,128)(2,1)S(1)} %collective-permute-done.1), dimensions={1} | concatenate | bytes 6488064 | tf_op jit(solution)/shard_map/concatenate | solution.py:22
  117.1 2.9 %fusion.8 = f32[1056]{0:T(1024)S(1)} fusion(bf16[1536,1056]{1,0:T(8,128)(2,1)} %concatenate.21), kind=kLoop, calls=%fused_computation.12 | loop fusion | flops 4864992 | bytes 3248256 | tf_op jit(solution)/shard_map/reduce_sum | solution.py:59
  120.1 0.1 copy-done.1
  120.2 0.0 copy-done.5
  120.2 3.7 %fusion.3 = bf16[1536,1056]{1,0:T(8,128)(2,1)S(1)} fusion(bf16[1536,1056]{1,0:T(8,128)(2,1)S(1)} %copy-done.1, f32[1056]{0:T(1024)S(1)} %add_rsqrt_fusion, f32[1536]{0:T(1024)S(1)} %copy-done.5), kind=kLoop, calls=%fused_computation.7 | loop fusion | flops 19464192 | bytes 6498432 | tf_op jit(solution)/shard_map/convert_element_type | solution.py:60
  123.9 0.0 copy-done.4
  123.9 1.1 fusion.13
  125.0 1.1 fusion.15
  126.2 0.0 copy-start.2
  126.2 0.0 copy-start.6
  126.2 1.1 fusion.17
  127.4 1.1 fusion.19
  128.5 0.0 copy-done.2
  128.5 0.0 copy-done.6
  128.5 0.0 copy-start.7
  128.5 0.0 copy-start.8
  128.5 0.7 fusion.47
  129.3 0.0 copy-start.3
  129.3 0.1 copy.21
  129.4 0.1 bitcast_reduce_fusion
  129.5 0.1 multiply_reduce_fusion
  129.6 1.0 fusion.61
  130.6 47.9 %all-reduce = (f32[64,64]{0,1:T(8,128)S(1)}, f32[64]{0:T(128)S(1)}) all-reduce(f32[64,64]{0,1:T(8,128)S(1)} %fusion.61, f32[64]{0:T(128)S(1)} %multiply_reduce_fusion), channel_id=1, replica_groups=mesh['row'=32,'col'=16] {'col'}, use_global_device_ids=true, to_apply=%region_2.3 | all-reduce | flops 4160 | bytes 33280 | tf_op jit(solution)/shard_map/psum | solution.py:82
  178.5 8.8 %collective-permute-start.2 = (bf16[64,32]{0,1:T(8,128)(2,1)S(1)}, bf16[64,32]{0,1:T(8,128)(2,1)S(1)}, u32[]{:S(2)}, u32[]{:S(2)}) collective-permute-start(bf16[64,32]{0,1:T(8,128)(2,1)S(1)} %get-tuple-element.7), channel_id=1, source_target_pairs={{0,16},{16,0},{32,48},{48,32},{64,80},{80,64},{96,112},{112,96},{1... | collective-permute-start | bytes 12296 | tf_op jit(solution)/shard_map/ppermute | solution.py:40
  187.3 0.8 collective-permute-done.2
  188.1 0.1 maximum_select_fusion.1
  188.2 9.4 %collective-permute-start.3 = (bf16[128,32]{0,1:T(8,128)(2,1)S(1)}, bf16[128,32]{0,1:T(8,128)(2,1)S(1)}, u32[]{:S(2)}, u32[]{:S(2)}) collective-permute-start(bf16[128,32]{0,1:T(8,128)(2,1)S(1)} %maximum_select_fusion.1), channel_id=1, source_target_pairs={{0,32},{32,0},{16,48},{48,16},{64,96},{96,64},{80,112},{112,80},{1... | collective-permute-start | bytes 24584 | tf_op jit(solution)/shard_map/ppermute | solution.py:40
  197.7 1.0 collective-permute-done.3
  198.7 4.7 %collective-permute-start.4 = (bf16[256,32]{0,1:T(8,128)(2,1)S(1)}, bf16[256,32]{0,1:T(8,128)(2,1)S(1)}, u32[]{:S(2)}, u32[]{:S(2)}) collective-permute-start(bf16[256,32]{0,1:T(8,128)(2,1)S(1)} %maximum_select_fusion), channel_id=1, source_target_pairs={{0,64},{64,0},{16,80},{80,16},{32,96},{96,32},{48,112},{112,48},{1... | collective-permute-start | bytes 49160 | tf_op jit(solution)/shard_map/ppermute | solution.py:40
  203.5 0.2 copy.23
  203.7 0.8 collective-permute-done.4
  204.5 0.1 fusion.65
  204.6 0.1 copy.24
  204.7 0.2 mul.101
  205.0 0.0 copy-done
  205.0 0.0 copy-done.7
  205.0 0.0 copy-done.8
  205.0 2.1 fusion.25
  207.0 0.0 copy-done.3
  (10 shorter events, 0.1 us)
Async XLA Ops:
  7.2 197.8 %copy-start = (bf16[1024,128]{1,0:T(8,128)(2,1)S(1)}, bf16[1024,128]{1,0:T(8,128)(2,1)}, u32[]{:S(2)}) copy-start(bf16[1024,128]{1,0:T(8,128)(2,1)} %param.14) | copy-start | bytes 786436
  7.2 76.0 %all-gather.2.cloned.1.call-start = ((), (), s32[]{:S(2)}) async-start(), calls=%async_computation | async-start | bytes 3342336 | tf_op jit(solution)/shard_map/all_gather | solution.py:56
  84.5 19.3 %collective-permute-start = (bf16[1536,16]{1,0:T(8,128)(2,1)S(1)}, bf16[1536,16]{1,0:T(8,128)(2,1)S(1)}, u32[]{:S(2)}, u32[]{:S(2)}) collective-permute-start(bf16[1536,16]{1,0:T(8,128)(2,1)S(1)} %get-tuple-element.5), channel_id=1, source_target_pairs={{0,16},{16,32},{32,48},{48,64},{64,80},{80,96},{96,112},{112,128},... | collective-permute-start | bytes 147464 | tf_op jit(solution)/shard_map/ppermute | solution.py:24
  99.0 10.6 %collective-permute-start.1 = (bf16[1536,16]{1,0:T(8,128)(2,1)S(1)}, bf16[1536,16]{1,0:T(8,128)(2,1)S(1)}, u32[]{:S(2)}, u32[]{:S(2)}) collective-permute-start(bf16[1536,16]{1,0:T(8,128)(2,1)S(1)} %get-tuple-element.4), channel_id=1, source_target_pairs={{16,0},{32,16},{48,32},{64,48},{80,64},{96,80},{112,96},{128,112},... | collective-permute-start | bytes 147464 | tf_op jit(solution)/shard_map/ppermute | solution.py:26
  117.1 3.1 %copy-start.1 = (bf16[1536,1056]{1,0:T(8,128)(2,1)S(1)}, bf16[1536,1056]{1,0:T(8,128)(2,1)}, u32[]{:S(2)}) copy-start(bf16[1536,1056]{1,0:T(8,128)(2,1)} %concatenate.21) | copy-start | bytes 9732100
  117.1 3.1 %copy-start.5 = (f32[1536]{0:T(1024)S(1)}, f32[1536]{0:T(1024)}, u32[]{:S(2)}) copy-start(f32[1536]{0:T(1024)} %param.11) | copy-start | bytes 18436
  120.2 3.7 %copy-start.4 = (bf16[5,96,1536]{2,1,0:T(8,128)(2,1)S(1)}, bf16[5,96,1536]{2,1,0:T(8,128)(2,1)}, u32[]{:S(2)}) copy-start(bf16[5,96,1536]{2,1,0:T(8,128)(2,1)} %param.9) | copy-start | bytes 4423684
  126.2 2.3 %copy-start.2 = (bf16[96,1024]{1,0:T(8,128)(2,1)S(1)}, bf16[96,1024]{1,0:T(8,128)(2,1)}, u32[]{:S(2)}) copy-start(bf16[96,1024]{1,0:T(8,128)(2,1)} %param.8) | copy-start | bytes 589828
  126.2 2.3 %copy-start.6 = (f32[96]{0:T(128)S(1)}, f32[96]{0:T(128)}, u32[]{:S(2)}) copy-start(f32[96]{0:T(128)} %param.10) | copy-start | bytes 1156
  128.5 76.5 %copy-start.7 = (bf16[64,32,128]{2,1,0:T(8,128)(2,1)S(1)}, bf16[64,32,128]{2,1,0:T(8,128)(2,1)}, u32[]{:S(2)}) copy-start(bf16[64,32,128]{2,1,0:T(8,128)(2,1)} %param.13) | copy-start | bytes 1572868
  128.5 76.5 %copy-start.8 = (f32[128]{0:T(128)S(1)}, f32[128]{0:T(128)}, u32[]{:S(2)}) copy-start(f32[128]{0:T(128)} %param.15) | copy-start | bytes 1540
  129.3 77.8 %copy-start.3 = (bf16[96,1024]{1,0:T(8,128)(2,1)}, bf16[96,1024]{1,0:T(8,128)(2,1)S(1)}, u32[]{:S(2)}) copy-start(bf16[96,1024]{1,0:T(8,128)(2,1)S(1)} %fusion.47) | copy-start | bytes 589828
  178.5 9.6 %collective-permute-start.2 = (bf16[64,32]{0,1:T(8,128)(2,1)S(1)}, bf16[64,32]{0,1:T(8,128)(2,1)S(1)}, u32[]{:S(2)}, u32[]{:S(2)}) collective-permute-start(bf16[64,32]{0,1:T(8,128)(2,1)S(1)} %get-tuple-element.7), channel_id=1, source_target_pairs={{0,16},{16,0},{32,48},{48,32},{64,80},{80,64},{96,112},{112,96},{1... | collective-permute-start | bytes 12296 | tf_op jit(solution)/shard_map/ppermute | solution.py:40
  188.2 10.5 %collective-permute-start.3 = (bf16[128,32]{0,1:T(8,128)(2,1)S(1)}, bf16[128,32]{0,1:T(8,128)(2,1)S(1)}, u32[]{:S(2)}, u32[]{:S(2)}) collective-permute-start(bf16[128,32]{0,1:T(8,128)(2,1)S(1)} %maximum_select_fusion.1), channel_id=1, source_target_pairs={{0,32},{32,0},{16,48},{48,16},{64,96},{96,64},{80,112},{112,80},{1... | collective-permute-start | bytes 24584 | tf_op jit(solution)/shard_map/ppermute | solution.py:40
  198.7 5.8 %collective-permute-start.4 = (bf16[256,32]{0,1:T(8,128)(2,1)S(1)}, bf16[256,32]{0,1:T(8,128)(2,1)S(1)}, u32[]{:S(2)}, u32[]{:S(2)}) collective-permute-start(bf16[256,32]{0,1:T(8,128)(2,1)S(1)} %maximum_select_fusion), channel_id=1, source_target_pairs={{0,64},{64,0},{16,80},{80,16},{32,96},{96,32},{48,112},{112,48},{1... | collective-permute-start | bytes 49160 | tf_op jit(solution)/shard_map/ppermute | solution.py:40
Sparse Core Ops, SparseCore 0:
  10.1 73.0 all-gather.1
where the time goes:
time: 215 us; the launch traced here: 214 us
  waiting for transfers between devices  87.2 us (41%)
  blocking collectives  47.9 us (22%)
  starting transfers between devices  39.5 us (18%)
  between operations  14.4 us (7%)
  local copies, waits for them, and re-layouts  9.64 us (4%)
  matrix products  8.25 us (4%)
  other arithmetic  7.03 us (3%)
    all_gather x1, waiting for transfers between devices, per_device(): gathered = lax.all_gather(trunk_in, 'col', axis=0, tiled=True)  75.2 us
    psum x1, blocking collectives, per_device(): lax.psum((partial_proj, jnp.sum(pooled_f * pooled_f, axis=0)), 'col')  47.9 us
    ppermute x3, starting transfers between devices, partner_2(): return lax.ppermute(block, axis, route)  23 us
    ppermute x1, starting transfers between devices, with_halo(): lax.ppermute(tail, axis, [(i, (i + 1) % count) for i in range(ends)])  14.6 us
    concatenate x1, local copies, waits for them, and re-layouts, with_halo(): jnp.concatenate([lax.ppermute(tail, axis, [(i, (i + 1) % count) for i in...  7.49 us
    ppermute x1, waiting for transfers between devices, with_halo(): lax.ppermute(head, axis, [((i + 1) % count, i) for i in range(ends)])  5.9 us
    dot_general x5, matrix products, per_device(): jnp.dot(conv_weight[tap_offset], gelu_output[:, tap_offset * DILATION_STE...  5.25 us
  transfers between devices with their start and end apart: 6, of which 6 were waited for; matrix products, arithmetic and copies ran while one was open for 0% of the time, Pallas kernels for 0%

commit v1 on v0

v1 whole, which is shorter than its diff:
```python
import functools
import jax
import jax.numpy as jnp
from jax import lax
from jax.experimental import pallas as pl
from jax.experimental.pallas import tpu as pltpu
from jax.sharding import PartitionSpec as P

MESH = pl.DeviceIdType.MESH
F32 = jnp.float32
BF16 = jnp.bfloat16

CH = 1536
OWN = 96
SEG = 512
EXT = 640
NY = 8
NROW = 32
TAPS = 5
STEP = 8
EPSILON = 1e-05


def gelu(v):
    u = 0.7978845608028654 * (v + 0.044715 * (v * v * v))
    return (0.5 * v) * (1.0 + jnp.tanh(u))


def kernel(
    x_hbm, w_hbm, cb_ref, g_ref, pp_ref, pair_hbm, opm_ref, pb_ref,
    tout_hbm, pout_hbm,
    xv, wbuf, raw_a, raw_b, swap, edge, stat, cbuf, act, gain, sc, taps, acc, bcol,
    tv, pool, zpool, part, side, cside, e1, e2, rexp, cexp, pin, pov,
    local_sem, pout_sem,
    swap_sem, cb_sem, edge_sem, ring_sem, stat_sem, w_sem, sib_sem, tout_sem, part_sem, side_sem,
):
    r = lax.axis_index("row")
    c = lax.axis_index("col")
    x = c // NY
    y = c % NY
    core = r % 2
    up = (r + 1) % NROW
    down = (r + NROW - 1) % NROW
    partner = (r, (1 - x) * NY + y)
    across = (r + 2 - 4 * ((r // 2) % 2), (1 - x) * NY + y)
    sibling = (r + 1 - 2 * core, c)
    ypeer = [(r, x * NY + (y + j) % NY) for j in range(NY)]
    dest = ((r // 8) * 8 + y, 2 * (r % 8) + x)
    source = ((r // 8) * 8 + c // 2, (c % 2) * NY + r % 8)
    to_self = jnp.logical_and(dest[0] == r, dest[1] == c)
    my_edge = r + 2 * x * 1 - 1
    my_edge = (my_edge + NROW) % NROW

    def send(src, dst, sems, dev):
        return pltpu.make_async_remote_copy(
            src_ref=src, dst_ref=dst, send_sem=sems.at[0], recv_sem=sems.at[1],
            device_id=dev, device_id_type=MESH,
        )

    half = pl.ds(pl.multiple_of(SEG * x, 128), SEG)
    load_x = pltpu.make_async_copy(x_hbm, xv, local_sem.at[0])
    load_a = pltpu.make_async_copy(x_hbm.at[:, half], raw_a.at[y], local_sem.at[1])
    load_w = pltpu.make_async_copy(
        w_hbm, wbuf.at[:, pl.ds(pl.multiple_of(OWN * x, 32), OWN), :], local_sem.at[2]
    )
    load_p = pltpu.make_async_copy(pair_hbm, pin, local_sem.at[3])
    load_x.start()
    load_a.start()

    barrier = pltpu.get_barrier_semaphore()
    greet = [partner, across, sibling] + ypeer[1:] + [(my_edge, y), (my_edge, NY + y)]
    for dev in greet:
        pl.semaphore_signal(barrier, inc=1, device_id=dev, device_id_type=MESH)

    @pl.when(jnp.logical_not(to_self))
    def _():
        pl.semaphore_signal(barrier, inc=1, device_id=source, device_id_type=MESH)

    cbuf[pl.ds(x, 1)] = jnp.broadcast_to(cb_ref[...], (1, 8, 128))
    load_x.wait()
    load_a.wait()
    pl.semaphore_wait(barrier, len(greet) + jnp.where(to_self, 0, 1))

    sent = []

    def go(copy):
        copy.start()
        sent.append(copy)
        return copy

    def ring(direction, kind, dist):
        buf = (raw_a, raw_b)[kind]
        if direction == 0:
            owner, dev = (y + NY - (dist - 1)) % NY, ypeer[1]
        else:
            owner, dev = (y + dist - 1) % NY, ypeer[NY - 1]
        return send(buf.at[owner], buf.at[owner], ring_sem.at[direction, kind, dist - 1], dev)

    def arrived(direction, kind, dist):
        buf = (raw_a, raw_b)[kind]
        owner = (y + NY - dist) % NY if direction == 0 else (y + dist) % NY
        send(buf.at[owner], buf.at[owner], ring_sem.at[direction, kind, dist - 1], ypeer[1]).wait_recv()

    other = 1 - x
    copy_swap = go(send(
        xv.at[:, pl.ds(pl.multiple_of(384 * other, 128), EXT)], swap, swap_sem, partner
    ))
    edge_up = send(xv.at[:, 896:1024], edge.at[x], edge_sem.at[x], (up, y))
    edge_down = send(xv.at[:, 0:128], edge.at[x], edge_sem.at[2 + x], (down, NY + y))
    edge_up.start()
    edge_down.start()
    go(ring(0, 0, 1))
    go(ring(1, 0, 1))
    copy_cb = go(send(cbuf.at[x], cbuf.at[x], cb_sem, partner))
    quarters = [pl.ds(pl.multiple_of(768 * core + 384 * q, 128), 384) for q in range(2)]
    mine = pl.ds(pl.multiple_of(OWN * x, 32), OWN)
    theirs = pl.ds(pl.multiple_of(OWN * other, 32), OWN)
    for q, dev in enumerate((partner, across)):
        go(send(w_hbm.at[:, :, quarters[q]], wbuf.at[:, mine, quarters[q]], w_sem.at[q], dev))
    load_w.start()
    load_p.start()

    copy_swap.wait_recv()
    for k in range(2):

        @pl.when(x == 0)
        def _():
            send(xv.at[:, 896:1024], edge.at[k], edge_sem.at[k], (up, y)).wait_recv()

        @pl.when(x == 1)
        def _():
            send(xv.at[:, 0:128], edge.at[k], edge_sem.at[2 + k], (up, y)).wait_recv()

    raw_b[y, 0:OWN, :] = swap[:, pl.ds(pl.multiple_of(128 * x, 128), SEG)]
    own_f = xv[:, half].astype(F32)
    their_f = raw_b[y, 0:OWN, :].astype(F32)
    sums = jnp.sum(own_f * own_f + their_f * their_f, axis=0, keepdims=True)
    at_end = jnp.logical_or(
        jnp.logical_and(x == 0, r == 0), jnp.logical_and(x == 1, r == NROW - 1)
    )
    lane = lax.broadcasted_iota(jnp.int32, (OWN, 128), 1)
    pick_inner = (lane < 64) == (x == 0)
    inner_a = xv[:, pl.ds(pl.multiple_of(SEG - 128 * x, 128), 128)].astype(F32)
    inner_b = swap[:, pl.ds(pl.multiple_of(SEG * other, 128), 128)].astype(F32)
    keep = jnp.where(at_end, 0.0, 1.0)
    outer_a = edge[x].astype(F32) * keep
    outer_b = edge[other].astype(F32) * keep
    halo_a = jnp.where(pick_inner, inner_a, outer_a)
    halo_b = jnp.where(pick_inner, inner_b, outer_b)
    halo_sums = jnp.sum(halo_a * halo_a + halo_b * halo_b, axis=0, keepdims=True)
    stat[y] = jnp.concatenate(
        [sums[:, 128 * t : 128 * t + 128] for t in range(4)]
        + [halo_sums, jnp.zeros((3, 128), F32)],
        axis=0,
    )
    for j in range(1, NY):
        go(send(stat.at[y], stat.at[y], stat_sem.at[j], ypeer[j]))
    lane48 = lax.broadcasted_iota(jnp.int32, (48, 128), 1)
    packed = halo_a[0:48]
    for q, piece in ((1, halo_a[48:96]), (2, halo_b[0:48]), (3, halo_b[48:96])):
        moved = pltpu.roll(piece, 32 * q, 1)
        inside = jnp.logical_and(lane48 >= 32 * q - 16, lane48 < 32 * q + 16)
        packed = jnp.where(inside, moved, packed)
    packed = packed.astype(BF16)
    for t in range(3):
        raw_b[y, OWN : OWN + 16, 128 * t : 128 * t + 128] = packed[16 * t : 16 * t + 16]
    raw_b[y, OWN : OWN + 16, 384:512] = jnp.zeros((16, 128), BF16)
    go(ring(0, 1, 1))
    go(ring(1, 1, 1))

    for i in range(12):
        gain[128 * i : 128 * i + 128, :] = jnp.transpose(
            jnp.broadcast_to(g_ref[i : i + 1, :], (128, 128))
        )
    arrived(0, 0, 1)
    go(ring(0, 0, 2))
    arrived(1, 0, 1)
    go(ring(1, 0, 2))
    token = lax.broadcasted_iota(jnp.int32, (SEG, 128), 0) // 16
    cell = lax.broadcasted_iota(jnp.int32, (SEG, 128), 1) % 32
    pool[...] = jnp.where(token == cell, 0.0625, 0.0).astype(BF16)
    zpool[...] = jnp.zeros(zpool.shape, BF16)
    entry = lax.broadcasted_iota(jnp.int32, (32, 1024), 0)
    column = lax.broadcasted_iota(jnp.int32, (32, 1024), 1)
    e1[...] = jnp.where(column // 32 == entry, 1.0, 0.0).astype(BF16)
    e2[...] = jnp.where(column % 32 == entry, 1.0, 0.0).astype(BF16)
    copy_cb.wait_recv()
    for k in range(2):
        bcol[OWN * k : OWN * k + OWN, :] = jnp.transpose(
            jnp.broadcast_to(cbuf[k, 0:1, :], (128, 128))
        )[0:OWN]

    total = stat[y]
    for j in range(1, NY):
        send(stat.at[y], stat.at[(y + NY - j) % NY], stat_sem.at[j], ypeer[j]).wait_recv()
        total = total + stat[(y + NY - j) % NY]
    sc[...] = lax.rsqrt(total * (1.0 / CH) + EPSILON)

    def first_row(kind, owner):
        return ((x if kind == 0 else other) * NY + owner) * OWN

    def activate(kind, owner):
        buf = (raw_a, raw_b)[kind]
        base = first_row(kind, owner)

        def body(b, carry):
            rows = pl.ds(pl.multiple_of(b * 32, 32), 32)
            target = pl.ds(pl.multiple_of(base + b * 32, 32), 32)
            g = gain[target, :]
            for t in range(4):
                cols = slice(128 * t, 128 * t + 128)
                v = buf[owner, rows, cols].astype(F32) * g * sc[t : t + 1, :]
                act[target, cols] = gelu(v).astype(BF16)
            return carry

        lax.fori_loop(0, 3, body, 0)

    def activate_halo(owner):
        block = jnp.concatenate(
            [
                raw_b[owner, OWN : OWN + 16, 128 * t : 128 * t + 128].astype(F32)
                for t in range(3)
            ],
            axis=0,
        )
        for q in range(4):
            piece = block if q == 0 else pltpu.roll(block, 128 - 32 * q, 1)
            base = first_row(q // 2, owner) + 48 * (q % 2)
            target = pl.ds(pl.multiple_of(base, 16), 48)
            v = piece * gain[target, :] * sc[4:5, :]
            act[target, SEG:EXT] = gelu(v).astype(BF16)

    def behind(d):
        return (y + NY - d) % NY

    def ahead(d):
        return (y + d) % NY

    arrived(0, 1, 1)
    go(ring(0, 1, 2))
    arrived(1, 1, 1)
    go(ring(1, 1, 2))
    activate(0, y)
    activate(1, y)
    activate_halo(y)
    activate(0, behind(1))
    activate(0, ahead(1))
    arrived(0, 0, 2)
    go(ring(0, 0, 3))
    arrived(1, 0, 2)
    go(ring(1, 0, 3))
    activate(1, behind(1))
    activate(1, ahead(1))
    activate_halo(behind(1))
    activate_halo(ahead(1))
    arrived(0, 1, 2)
    go(ring(0, 1, 3))
    arrived(1, 1, 2)
    go(ring(1, 1, 3))
    activate(0, behind(2))
    activate(0, ahead(2))
    arrived(0, 0, 3)
    go(ring(0, 0, 4))
    arrived(1, 0, 3)
    for q in range(2):
        send(
            w_hbm.at[:, :, quarters[q]], wbuf.at[:, theirs, quarters[q]], w_sem.at[q], partner
        ).wait_recv()
    k_half = pl.ds(pl.multiple_of(768 * core, 128), 768)
    k_rest = pl.ds(pl.multiple_of(768 * (1 - core), 128), 768)
    go(send(wbuf.at[:, theirs, k_half], wbuf.at[:, theirs, k_half], sib_sem, sibling))
    activate(1, behind(2))
    activate(1, ahead(2))
    activate_halo(behind(2))
    activate_halo(ahead(2))
    activate(0, behind(3))
    activate(0, ahead(3))
    arrived(0, 1, 3)
    arrived(1, 1, 3)
    go(ring(1, 1, 4))
    activate(1, behind(3))
    activate(1, ahead(3))
    activate_halo(behind(3))
    activate_halo(ahead(3))
    load_w.wait()
    send(wbuf.at[:, theirs, k_rest], wbuf.at[:, theirs, k_rest], sib_sem, sibling).wait_recv()

    def product(tap, group):
        out = None
        for k in range(2):
            span = pl.ds(pl.multiple_of(768 * k + 384 * group, 128), 384)
            term = jnp.dot(wbuf[tap, :, span], act[span, :], preferred_element_type=F32)
            out = term if out is None else out + term
        return out

    group = y // 4

    def early(tap, carry):
        taps[tap] = product(tap, group)
        return carry

    lax.fori_loop(0, TAPS, early, 0)

    arrived(0, 0, 4)
    activate(0, behind(4))
    arrived(1, 1, 4)
    activate(1, ahead(4))
    activate_halo(ahead(4))

    for tap in range(TAPS):
        full = taps[tap] + product(tap, 1 - group)
        delta = STEP * (tap - 2)
        if delta != 0:
            full = pltpu.roll(full, (-delta) % EXT, 1)
        full = full[:, 0:SEG]
        if tap == 0:
            acc[...] = full
        else:
            acc[...] += full

    for t in range(4):
        cols = slice(128 * t, 128 * t + 128)
        own_cols = pl.ds(pl.multiple_of(SEG * x + 128 * t, 128), 128)
        tv[mine, cols] = (
            xv[:, own_cols].astype(F32) + acc[mine, cols] + bcol[mine, :]
        ).astype(BF16)
        tv[theirs, cols] = (
            raw_b[y, 0:OWN, cols].astype(F32) + acc[theirs, cols] + bcol[theirs, :]
        ).astype(BF16)
    copy_t = go(send(tv.at[theirs, :], tout_hbm.at[:, half], tout_sem, partner))
    store_t = pltpu.make_async_copy(tv.at[mine, :], tout_hbm.at[:, half], local_sem.at[4])
    store_t.start()
    pooled = jnp.dot(tv[...], pool[...], preferred_element_type=F32).astype(BF16)
    zpool[pl.ds(pl.multiple_of(OWN * y, 32), OWN), :] = pooled[0:OWN]
    zpool[pl.ds(pl.multiple_of(768 + OWN * y, 32), OWN), :] = pooled[OWN:]
    pooled_f = pooled.astype(F32)
    squares = jnp.sum(pooled_f * pooled_f, axis=0, keepdims=True)
    proj = jnp.dot(pp_ref[...], zpool[...], preferred_element_type=F32)
    lane16 = lax.broadcasted_iota(jnp.int32, (16, 128), 1) // 32
    folded = proj[0:16]
    for q in range(1, 4):
        folded = jnp.where(lane16 == q, proj[16 * q : 16 * q + 16], folded)
    part[y] = jnp.concatenate([folded, jnp.broadcast_to(squares, (8, 128))], axis=0)
    for j in range(1, NY):
        go(send(part.at[y], part.at[y], part_sem.at[j], ypeer[j]))
    whole = part[y]
    load_p.wait()
    for j in range(1, NY):
        frm = (y + NY - j) % NY
        send(part.at[y], part.at[frm], part_sem.at[j], ypeer[j]).wait_recv()
        whole = whole + part[frm]
    norm = lax.rsqrt(whole[16:17] * (1.0 / CH) + EPSILON)
    sides = (whole[0:16] * norm).astype(BF16)
    side[x] = sides
    copy_side = go(send(side.at[x], side.at[x], side_sem.at[0], partner))
    copy_c = send(side.at[x], cside, side_sem.at[1], dest)

    @pl.when(jnp.logical_not(to_self))
    def _():
        copy_c.start()

    copy_side.wait_recv()
    s0 = side[0].astype(F32)
    s1 = side[1].astype(F32)
    low = lax.broadcasted_iota(jnp.int32, (16, 128), 1) < 32
    row_t = jnp.concatenate(
        [
            jnp.where(low, s0, pltpu.roll(s1, 32, 1)),
            jnp.where(low, pltpu.roll(s0, 96, 1), s1),
        ],
        axis=0,
    )
    row_side = jnp.transpose(row_t)[0:64].astype(BF16)
    rexp[...] = jnp.dot(row_side, e1[...], preferred_element_type=F32)

    @pl.when(jnp.logical_not(to_self))
    def _():
        copy_c.wait_recv()

    @pl.when(to_self)
    def _():
        cside[...] = side[x]

    cs = cside[...].astype(F32)
    col_t = jnp.concatenate([pltpu.roll(cs, 64, 1), pltpu.roll(cs, 32, 1)], axis=0)
    col_side = jnp.transpose(col_t)[0:32].astype(BF16)
    cexp[...] = jnp.dot(col_side, e2[...], preferred_element_type=F32)

    def block(b, carry):
        rows = pl.ds(pl.multiple_of(b * 8, 8), 8)
        outer = jnp.concatenate(
            [(rexp[pl.ds(b * 8 + i, 1), :] * cexp[...]).astype(BF16) for i in range(8)], axis=0
        )
        update = jnp.dot(outer, opm_ref[...], preferred_element_type=F32)
        update = update.reshape(8, 32, 128)
        pov[rows] = (pin[rows].astype(F32) + update + pb_ref[...].reshape(1, 1, 128)).astype(BF16)
        pltpu.make_async_copy(pov.at[rows], pout_hbm.at[rows], pout_sem.at[b]).start()
        return carry

    lax.fori_loop(0, 8, block, 0)

    for b in range(8):
        rows = pl.ds(8 * b, 8)
        pltpu.make_async_copy(pov.at[rows], pout_hbm.at[rows], pout_sem.at[b]).wait()
    store_t.wait()
    other_half = pl.ds(pl.multiple_of(SEG * other, 128), SEG)
    send(tv.at[theirs, :], tout_hbm.at[:, other_half], tout_sem, partner).wait_recv()
    for copy in sent:
        copy.wait_send()
    edge_up.wait_send()
    edge_down.wait_send()

    @pl.when(jnp.logical_not(to_self))
    def _():
        copy_c.wait_send()


def per_device(trunk_in, conv_weight, conv_bias, norm_gain, pair_proj, pair_in, opm_weight, pair_bias):
    any_spec = pl.BlockSpec(memory_space=pl.ANY)
    vmem = pl.BlockSpec(memory_space=pltpu.VMEM)
    dma = pltpu.SemaphoreType.DMA
    bias_row = jnp.pad(conv_bias, (0, 128 - OWN)).reshape(1, 128)
    return pl.pallas_call(
        kernel,
        name="trunk_pair",
        out_shape=(
            jax.ShapeDtypeStruct(trunk_in.shape, BF16),
            jax.ShapeDtypeStruct(pair_in.shape, BF16),
        ),
        in_specs=[any_spec, any_spec, vmem, vmem, vmem, any_spec, vmem, vmem],
        out_specs=(any_spec, any_spec),
        scratch_shapes=[
            pltpu.VMEM((OWN, 1024), BF16),
            pltpu.VMEM((TAPS, 2 * OWN, CH), BF16),
            pltpu.VMEM((NY, OWN, SEG), BF16),
            pltpu.VMEM((NY, OWN + 16, SEG), BF16),
            pltpu.VMEM((OWN, EXT), BF16),
            pltpu.VMEM((2, OWN, 128), BF16),
            pltpu.VMEM((NY, 8, 128), F32),
            pltpu.VMEM((2, 8, 128), F32),
            pltpu.VMEM((CH, EXT), BF16),
            pltpu.VMEM((CH, 128), F32),
            pltpu.VMEM((8, 128), F32),
            pltpu.VMEM((TAPS, 2 * OWN, EXT), F32),
            pltpu.VMEM((2 * OWN, SEG), F32),
            pltpu.VMEM((2 * OWN, 128), F32),
            pltpu.VMEM((2 * OWN, SEG), BF16),
            pltpu.VMEM((SEG, 128), BF16),
            pltpu.VMEM((CH, 128), BF16),
            pltpu.VMEM((NY, 24, 128), F32),
            pltpu.VMEM((2, 16, 128), BF16),
            pltpu.VMEM((16, 128), BF16),
            pltpu.VMEM((32, 1024), BF16),
            pltpu.VMEM((32, 1024), BF16),
            pltpu.VMEM((64, 1024), F32),
            pltpu.VMEM((32, 1024), F32),
            pltpu.VMEM((64, 32, 128), BF16),
            pltpu.VMEM((64, 32, 128), BF16),
            dma((5,)),
            dma((8,)),
            dma((2,)),
            dma((2,)),
            dma((4, 2)),
            dma((2, 2, 4, 2)),
            dma((NY, 2)),
            dma((2, 2)),
            dma((2,)),
            dma((2,)),
            dma((NY, 2)),
            dma((2, 2)),
        ],
        compiler_params=pltpu.CompilerParams(
            collective_id=0, has_side_effects=True, vmem_limit_bytes=48 * 1024 * 1024
        ),
        cost_estimate=pl.CostEstimate(
            flops=2_000_000_000, bytes_accessed=4_000_000, transcendentals=1_000_000
        ),
    )(
        trunk_in, conv_weight, bias_row, norm_gain.reshape(12, 128), pair_proj, pair_in,
        opm_weight, pair_bias.reshape(1, 128),
    )


def solution(mesh):
    return jax.shard_map(
        per_device,
        mesh=mesh,
        in_specs=(
            P("col", "row"), P(None, "col", None), P("col"), P(), P(), P("row", "col", None), P(), P(),
        ),
        out_specs=(P("col", "row"), P("row", "col", None)),
        check_vma=False,
    )
```

time: 215 us -> 63.1 us (0.29)
  waiting for transfers between devices: 87.2 us -> 0 us
  Pallas kernels: 0 us -> 53 us
  blocking collectives: 47.9 us -> 0 us
  starting transfers between devices: 39.5 us -> 0 us
  between operations: 14.4 us -> 0.65 us
  matrix products: 8.25 us -> 0 us
  other arithmetic: 7.03 us -> 0 us
    all_gather x1 -> x0, waiting for transfers between devices: 75.2 us -> none  [per_device(): gathered = lax.all_gather(trunk_in, 'col', axis=0, tiled=True)]
    pallas_call x0 -> x1, Pallas kernels: none -> 53 us  [per_device(): pl.pallas_call(kernel, name='trunk_pair', out_shape=(jax.ShapeDtypeStruct...]
    psum x1 -> x0, blocking collectives: 47.9 us -> none  [per_device(): lax.psum((partial_proj, jnp.sum(pooled_f * pooled_f, axis=0)), 'col')]
    ppermute x5 -> x0, starting transfers between devices: 39.5 us -> none  [the longest x3 23 us: partner_2(): return lax.ppermute(block, axis, route)]
    ppermute x5 -> x0, waiting for transfers between devices: 11.3 us -> none  [the longest x1 5.9 us: with_halo(): lax.ppermute(head, axis, [((i + 1) % count, i) for i in range(ends)])]
    dot_general x7 -> x0, matrix products: 8.25 us -> none  [the longest x5 5.25 us: per_device(): jnp.dot(conv_weight[tap_offset], gelu_output[:, tap_offset * DILATION_STE...]
    unnamed x18 -> x16, local copies, waits for them, and re-layouts: 0.17 us -> 8.04 us
    concatenate x1 -> x0, local copies, waits for them, and re-layouts: 7.49 us -> none  [with_halo(): jnp.concatenate([lax.ppermute(tail, axis, [(i, (i + 1) % count) for i in...]
  transfers between devices with their start and end apart: 6 -> 0, of which waited for: 6 -> 0; matrix products, arithmetic and copies ran while one was open for 0% -> 0% of each run, Pallas kernels for 0% -> 0%
where the time goes in v1:
time: 63.1 us; the launch traced here: 62.4 us
  Pallas kernels  53 us (84%)
  local copies, waits for them, and re-layouts  8.7 us (14%)
  between operations  0.65 us (1%)
    pallas_call x1, Pallas kernels, per_device(): pl.pallas_call(kernel, name='trunk_pair', out_shape=(jax.ShapeDtypeStruct...  53 us
    unnamed x16, local copies, waits for them, and re-layouts  8.04 us

profile of v1, /device:TPU:1, one launch (start us, length us, event | category | flops | bytes accessed | tf_op | source)
XLA Modules:
  0.0 62.4 jit_solution(8677968746620677092)
XLA Ops:
  0.6 0.7 %pad_bitcast_fusion.cb_ref = f32[1,128]{1,0:T(1,128)S(1)} fusion(f32[96]{0:T(128)} %param.10), kind=kLoop, calls=%fused_computation | loop fusion | bytes 896 | tf_op jit(solution)/shard_map/reshape | solution.py:422
  1.3 0.0 copy-start
  1.3 1.4 %copy-done = bf16[5,96,1536]{2,1,0:T(8,128)(2,1)S(1)} copy-done((bf16[5,96,1536]{2,1,0:T(8,128)(2,1)S(1)}, bf16[5,96,1536]{2,1,0:T(8,128)(2,1)}, u32[]{:S(2)}) %copy-start) | copy-done | bytes 1474584
  2.7 0.0 copy-start.1
  2.7 1.0 %copy-done.1 = bf16[64,32,128]{2,1,0:T(8,128)(2,1)S(1)} copy-done((bf16[64,32,128]{2,1,0:T(8,128)(2,1)S(1)}, bf16[64,32,128]{2,1,0:T(8,128)(2,1)}, u32[]{:S(2)}) %copy-start.1) | copy-done | bytes 524312
  3.7 0.0 copy-start.2
  3.7 0.9 %copy-done.2 = bf16[1024,128]{1,0:T(8,128)(2,1)S(1)} copy-done((bf16[1024,128]{1,0:T(8,128)(2,1)S(1)}, bf16[1024,128]{1,0:T(8,128)(2,1)}, u32[]{:S(2)}) %copy-start.2) | copy-done | bytes 262168
  4.7 0.0 copy-start.3
  4.7 0.9 %copy-done.3 = bf16[96,1024]{1,0:T(8,128)(2,1)S(1)} copy-done((bf16[96,1024]{1,0:T(8,128)(2,1)S(1)}, bf16[96,1024]{1,0:T(8,128)(2,1)}, u32[]{:S(2)}) %copy-start.3) | copy-done | bytes 196632
  5.6 0.0 copy-start.4
  5.6 0.9 %copy-done.4 = bf16[64,1536]{1,0:T(8,128)(2,1)S(1)} copy-done((bf16[64,1536]{1,0:T(8,128)(2,1)S(1)}, bf16[64,1536]{1,0:T(8,128)(2,1)}, u32[]{:S(2)}) %copy-start.4) | copy-done | bytes 196632
  6.5 0.0 copy-start.5
  6.5 0.7 %copy-done.5 = f32[1536]{0:T(1024)S(1)} copy-done((f32[1536]{0:T(1024)S(1)}, f32[1536]{0:T(1024)}, u32[]{:S(2)}) %copy-start.5) | copy-done | bytes 6168
  7.2 0.0 copy-start.6
  7.2 0.7 %copy-done.6 = f32[128]{0:T(128)S(1)} copy-done((f32[128]{0:T(128)S(1)}, f32[128]{0:T(128)}, u32[]{:S(2)}) %copy-start.6) | copy-done | bytes 536
  7.9 53.0 %trunk_pair.1 = (bf16[96,1024]{1,0:T(8,128)(2,1)S(1)}, bf16[64,32,128]{2,1,0:T(8,128)(2,1)S(1)}) custom-call(bf16[96,1024]{1,0:T(8,128)(2,1)S(1)} %copy-done.3, bf16[5,96,1536]{2,1,0:T(8,128)(2,1)S(1)} %copy-done, f32[1,128]{1,0:T(1,128)S(1)} %pad_bitcast_fusion.cb_ref, f32[12,128]{1,0:T(8,128)S(1)} %bitcast.4, bf16[64,1536]{1,0:T(8,128)(2,1)S(1)} %copy-done.4, ...), custom_call_target="tpu_custom_call" | custom-call | flops 2000000000 | bytes 4000000 | tf_op jit(solution)/shard_map/trunk_pair/pallas_call | solution.py:423
  60.9 0.7 %copy.12 = bf16[96,1024]{1,0:T(8,128)(2,1)} copy(bf16[96,1024]{1,0:T(8,128)(2,1)S(1)} %get-tuple-element.4) | data formatting | bytes 393216
  61.6 0.8 %copy.13 = bf16[64,32,128]{2,1,0:T(8,128)(2,1)} copy(bf16[64,32,128]{2,1,0:T(8,128)(2,1)S(1)} %get-tuple-element.5) | data formatting | bytes 1048576
Async XLA Ops:
  1.3 1.4 %copy-start = (bf16[5,96,1536]{2,1,0:T(8,128)(2,1)S(1)}, bf16[5,96,1536]{2,1,0:T(8,128)(2,1)}, u32[]{:S(2)}) copy-start(bf16[5,96,1536]{2,1,0:T(8,128)(2,1)} %w_hbm.1) | copy-start | bytes 4423684
  2.7 1.0 %copy-start.1 = (bf16[64,32,128]{2,1,0:T(8,128)(2,1)S(1)}, bf16[64,32,128]{2,1,0:T(8,128)(2,1)}, u32[]{:S(2)}) copy-start(bf16[64,32,128]{2,1,0:T(8,128)(2,1)} %pair_hbm.1) | copy-start | bytes 1572868
  3.7 0.9 %copy-start.2 = (bf16[1024,128]{1,0:T(8,128)(2,1)S(1)}, bf16[1024,128]{1,0:T(8,128)(2,1)}, u32[]{:S(2)}) copy-start(bf16[1024,128]{1,0:T(8,128)(2,1)} %opm_ref.1) | copy-start | bytes 786436
  4.7 0.9 %copy-start.3 = (bf16[96,1024]{1,0:T(8,128)(2,1)S(1)}, bf16[96,1024]{1,0:T(8,128)(2,1)}, u32[]{:S(2)}) copy-start(bf16[96,1024]{1,0:T(8,128)(2,1)} %x_hbm.1) | copy-start | bytes 589828
  5.6 0.9 %copy-start.4 = (bf16[64,1536]{1,0:T(8,128)(2,1)S(1)}, bf16[64,1536]{1,0:T(8,128)(2,1)}, u32[]{:S(2)}) copy-start(bf16[64,1536]{1,0:T(8,128)(2,1)} %pp_ref.1) | copy-start | bytes 589828
  6.5 0.7 %copy-start.5 = (f32[1536]{0:T(1024)S(1)}, f32[1536]{0:T(1024)}, u32[]{:S(2)}) copy-start(f32[1536]{0:T(1024)} %param.11) | copy-start | bytes 18436
  7.2 0.7 %copy-start.6 = (f32[128]{0:T(128)S(1)}, f32[128]{0:T(128)}, u32[]{:S(2)}) copy-start(f32[128]{0:T(128)} %param.15) | copy-start | bytes 1540

commit v2 on v1

v2 whole, which is shorter than its diff:
```python
import functools
import jax
import jax.numpy as jnp
from jax import lax
from jax.experimental import pallas as pl
from jax.experimental.pallas import tpu as pltpu
from jax.sharding import PartitionSpec as P

MESH = pl.DeviceIdType.MESH
F32 = jnp.float32
BF16 = jnp.bfloat16

CH = 1536
OWN = 96
SEG = 512
EXT = 640
NY = 8
NROW = 32
TAPS = 5
STEP = 8
EPSILON = 1e-05


def gelu(v):
    u = 0.7978845608028654 * (v + 0.044715 * (v * v * v))
    return (0.5 * v) * (1.0 + jnp.tanh(u))


def kernel(
    x_hbm, w_hbm, cb_hbm, g_hbm, pp_hbm, opm_hbm,
    tout_hbm, sides_hbm, wide_hbm,
    xv, wbuf, raw_a, raw_b, swap, edge, hal, cbuf, act, gain, sc, taps, acc, bcol,
    tv, pool, zpool, part, side, cb_ref, g_ref, pp_ref, opm_ref, opm_f, wide,
    local_sem,
    swap_sem, cb_sem, edge_sem, ring_sem, hal_sem, w_sem, sib_sem, tout_sem, part_sem, side_sem,
):
    r = lax.axis_index("row")
    c = lax.axis_index("col")
    x = c // NY
    y = c % NY
    core = r % 2
    up = (r + 1) % NROW
    down = (r + NROW - 1) % NROW
    partner = (r, (1 - x) * NY + y)
    across = (r + 2 - 4 * ((r // 2) % 2), (1 - x) * NY + y)
    sibling = (r + 1 - 2 * core, c)
    ypeer = [(r, x * NY + (y + j) % NY) for j in range(NY)]
    dest = ((r // 8) * 8 + y, 2 * (r % 8) + x)
    source = ((r // 8) * 8 + c // 2, (c % 2) * NY + r % 8)
    to_self = jnp.logical_and(dest[0] == r, dest[1] == c)
    my_edge = r + 2 * x * 1 - 1
    my_edge = (my_edge + NROW) % NROW

    def send(src, dst, sems, dev):
        return pltpu.make_async_remote_copy(
            src_ref=src, dst_ref=dst, send_sem=sems.at[0], recv_sem=sems.at[1],
            device_id=dev, device_id_type=MESH,
        )

    half = pl.ds(pl.multiple_of(SEG * x, 128), SEG)
    load_x = pltpu.make_async_copy(x_hbm, xv, local_sem.at[0])
    load_a = pltpu.make_async_copy(x_hbm.at[:, half], raw_a.at[y], local_sem.at[1])
    load_w = pltpu.make_async_copy(
        w_hbm, wbuf.at[:, pl.ds(pl.multiple_of(OWN * x, 32), OWN), :], local_sem.at[2]
    )
    tables = [
        pltpu.make_async_copy(src, dst, local_sem.at[5 + k])
        for k, (src, dst) in enumerate(
            ((cb_hbm, cb_ref), (g_hbm, g_ref), (pp_hbm, pp_ref), (opm_hbm, opm_ref))
        )
    ]
    load_x.start()
    load_a.start()
    for copy in tables[:2]:
        copy.start()

    barrier = pltpu.get_barrier_semaphore()
    diagonal = [(r, (1 - x) * NY + (y + j) % NY) for j in (1, NY - 1)]
    greet = [partner, across, sibling] + diagonal + ypeer[1:] + [(my_edge, y), (my_edge, NY + y)]
    for dev in greet:
        pl.semaphore_signal(barrier, inc=1, device_id=dev, device_id_type=MESH)

    @pl.when(jnp.logical_not(to_self))
    def _():
        pl.semaphore_signal(barrier, inc=1, device_id=source, device_id_type=MESH)

    cbuf[pl.ds(x, 1)] = jnp.zeros((1, 8, 128), F32)
    tables[0].wait()
    cbuf[pl.ds(x, 1), :, 0:OWN] = jnp.broadcast_to(cb_ref[...].reshape(1, 1, OWN), (1, 8, OWN))
    load_x.wait()
    load_a.wait()
    pl.semaphore_wait(barrier, len(greet) + jnp.where(to_self, 0, 1))

    sent = []

    def go(copy):
        copy.start()
        sent.append(copy)
        return copy

    def piece_of(kind, owner, piece):
        return (raw_a, raw_b)[kind].at[owner, 48 * piece : 48 * piece + 48]

    def ring(direction, kind, dist, piece):
        owner = (y + NY - (dist - 1)) % NY if direction == 0 else (y + dist - 1) % NY
        at = piece_of(kind, owner, piece)
        dev = ypeer[1] if direction == 0 else ypeer[NY - 1]
        src = at
        if kind == 1 and dist == 1:
            src = xv.at[48 * piece : 48 * piece + 48, other_half]
            dev = diagonal[direction]
        return send(src, at, ring_sem.at[direction, kind, dist - 1, piece], dev)

    def arrived(direction, kind, dist, piece):
        owner = (y + NY - dist) % NY if direction == 0 else (y + dist) % NY
        at = piece_of(kind, owner, piece)
        send(at, at, ring_sem.at[direction, kind, dist - 1, piece], ypeer[1]).wait_recv()

    def step(kind, dist, piece):
        if dist < 4 or kind == 0:
            arrived(0, kind, dist, piece)
            if dist < 3 or (dist == 3 and kind == 0):
                go(ring(0, kind, dist + 1, piece))
        if dist < 4 or kind == 1:
            arrived(1, kind, dist, piece)
            if dist < 3 or (dist == 3 and kind == 1):
                go(ring(1, kind, dist + 1, piece))

    other_half = pl.ds(pl.multiple_of(SEG * (1 - x), 128), SEG)
    other = 1 - x
    edge_up = send(xv.at[:, 896:1024], edge.at[x], edge_sem.at[x], (up, y))
    edge_down = send(xv.at[:, 0:128], edge.at[x], edge_sem.at[2 + x], (down, NY + y))
    edge_up.start()
    edge_down.start()
    for piece in range(2):
        for direction in range(2):
            go(ring(direction, 0, 1, piece))
    copy_swap = go(send(
        xv.at[:, pl.ds(pl.multiple_of(384 * other, 128), EXT)], swap, swap_sem, partner
    ))
    for piece in range(2):
        for direction in range(2):
            go(ring(direction, 1, 1, piece))
    copy_cb = go(send(cbuf.at[x], cbuf.at[x], cb_sem, partner))
    quarters = [pl.ds(pl.multiple_of(768 * core + 384 * q, 128), 384) for q in range(2)]
    mine = pl.ds(pl.multiple_of(OWN * x, 32), OWN)
    theirs = pl.ds(pl.multiple_of(OWN * other, 32), OWN)
    for q, dev in enumerate((partner, across)):
        go(send(w_hbm.at[:, :, quarters[q]], wbuf.at[:, mine, quarters[q]], w_sem.at[q], dev))
    load_w.start()
    for copy in tables[2:]:
        copy.start()

    tables[1].wait()
    for i in range(12):
        gain[128 * i : 128 * i + 128, :] = jnp.transpose(
            jnp.broadcast_to(g_ref[i : i + 1, :], (128, 128))
        )
    for piece in range(2):
        step(0, 1, piece)

    copy_swap.wait_recv()
    for k in range(2):

        @pl.when(x == 0)
        def _():
            send(xv.at[:, 896:1024], edge.at[k], edge_sem.at[k], (up, y)).wait_recv()

        @pl.when(x == 1)
        def _():
            send(xv.at[:, 0:128], edge.at[k], edge_sem.at[2 + k], (up, y)).wait_recv()

    raw_b[y, 0:OWN, :] = swap[:, pl.ds(pl.multiple_of(128 * x, 128), SEG)]
    own_f = xv[:, half].astype(F32)
    their_f = raw_b[y, 0:OWN, :].astype(F32)
    sums = jnp.sum(own_f * own_f + their_f * their_f, axis=0, keepdims=True)
    at_end = jnp.logical_or(
        jnp.logical_and(x == 0, r == 0), jnp.logical_and(x == 1, r == NROW - 1)
    )
    lane = lax.broadcasted_iota(jnp.int32, (OWN, 128), 1)
    pick_inner = (lane < 64) == (x == 0)
    inner_a = xv[:, pl.ds(pl.multiple_of(SEG - 128 * x, 128), 128)].astype(F32)
    inner_b = swap[:, pl.ds(pl.multiple_of(SEG * other, 128), 128)].astype(F32)
    keep = jnp.where(at_end, 0.0, 1.0)
    outer_a = edge[x].astype(F32) * keep
    outer_b = edge[other].astype(F32) * keep
    halo_a = jnp.where(pick_inner, inner_a, outer_a)
    halo_b = jnp.where(pick_inner, inner_b, outer_b)
    halo_sums = jnp.sum(halo_a * halo_a + halo_b * halo_b, axis=0, keepdims=True)
    lane48 = lax.broadcasted_iota(jnp.int32, (48, 128), 1)
    packed = halo_a[0:48]
    for q, piece in ((1, halo_a[48:96]), (2, halo_b[0:48]), (3, halo_b[48:96])):
        moved = pltpu.roll(piece, 32 * q, 1)
        inside = jnp.logical_and(lane48 >= 32 * q - 16, lane48 < 32 * q + 16)
        packed = jnp.where(inside, moved, packed)
    sums = jnp.concatenate(
        [sums[:, 128 * t : 128 * t + 128] for t in range(4)]
        + [halo_sums, jnp.zeros((3, 128), F32)],
        axis=0,
    )
    rest = sums - sums.astype(BF16).astype(F32)
    hal[y] = jnp.concatenate([packed, sums, rest], axis=0).astype(BF16)
    for j in range(1, NY):
        go(send(hal.at[y], hal.at[y], hal_sem.at[j], ypeer[j]))
    for piece in range(2):
        step(1, 1, piece)
    token = lax.broadcasted_iota(jnp.int32, (SEG, 128), 0) // 16
    cell = lax.broadcasted_iota(jnp.int32, (SEG, 128), 1) % 32
    pool[...] = jnp.where(token == cell, 0.0625, 0.0).astype(BF16)
    zpool[...] = jnp.zeros(zpool.shape, BF16)
    tables[3].wait()
    opm_f[...] = opm_ref[...].astype(F32)
    for v in range(32):
        wide[:, 128 * v : 128 * v + 128] = opm_f[pl.ds(v, 32, stride=32), :].astype(BF16)
    store_wide = pltpu.make_async_copy(wide, wide_hbm, local_sem.at[3])
    store_wide.start()
    copy_cb.wait_recv()
    for k in range(2):
        bcol[OWN * k : OWN * k + OWN, :] = jnp.transpose(
            jnp.broadcast_to(cbuf[k, 0:1, :], (128, 128))
        )[0:OWN]

    for piece in range(2):
        step(0, 2, piece)

    def sums_of(owner):
        both = hal[owner, 48:64, :].astype(F32)
        return both[0:8] + both[8:16]

    total = sums_of(y)
    for j in range(1, NY):
        frm = (y + NY - j) % NY
        send(hal.at[y], hal.at[frm], hal_sem.at[j], ypeer[j]).wait_recv()
        total = total + sums_of(frm)
    sc[...] = lax.rsqrt(total * (1.0 / CH) + EPSILON)

    def first_row(kind, owner):
        return ((x if kind == 0 else other) * NY + owner) * OWN

    def activate(kind, owner):
        buf = (raw_a, raw_b)[kind]
        base = first_row(kind, owner)

        def body(b, carry):
            rows = pl.ds(pl.multiple_of(b * 32, 32), 32)
            target = pl.ds(pl.multiple_of(base + b * 32, 32), 32)
            g = gain[target, :]
            for t in range(4):
                cols = slice(128 * t, 128 * t + 128)
                v = buf[owner, rows, cols].astype(F32) * g * sc[t : t + 1, :]
                act[target, cols] = gelu(v).astype(BF16)
            return carry

        lax.fori_loop(0, 3, body, 0)

    def activate_halo(owner):
        block = hal[owner, 0:48, :].astype(F32)
        for q in range(4):
            piece = block if q == 0 else pltpu.roll(block, 128 - 32 * q, 1)
            base = first_row(q // 2, owner) + 48 * (q % 2)
            target = pl.ds(pl.multiple_of(base, 16), 48)
            v = piece * gain[target, :] * sc[4:5, :]
            act[target, SEG:EXT] = gelu(v).astype(BF16)

    def behind(d):
        return (y + NY - d) % NY

    def ahead(d):
        return (y + d) % NY

    activate(0, y)
    activate(1, y)
    for piece in range(2):
        step(1, 2, piece)
    activate_halo(y)
    for owner in (behind(1), ahead(1)):
        activate(0, owner)
        activate(1, owner)
    for piece in range(2):
        step(0, 3, piece)
    for owner in (behind(1), ahead(1)):
        activate_halo(owner)
    for owner in (behind(2), ahead(2)):
        activate(0, owner)
    for piece in range(2):
        step(1, 3, piece)
    for q in range(2):
        send(
            w_hbm.at[:, :, quarters[q]], wbuf.at[:, theirs, quarters[q]], w_sem.at[q], partner
        ).wait_recv()
    k_half = pl.ds(pl.multiple_of(768 * core, 128), 768)
    k_rest = pl.ds(pl.multiple_of(768 * (1 - core), 128), 768)
    go(send(wbuf.at[:, theirs, k_half], wbuf.at[:, theirs, k_half], sib_sem, sibling))
    for owner in (behind(2), ahead(2)):
        activate(1, owner)
        activate_halo(owner)
    for owner in (behind(3), ahead(3)):
        activate(0, owner)
        activate(1, owner)
        activate_halo(owner)
    activate_halo(ahead(4))
    load_w.wait()
    send(wbuf.at[:, theirs, k_rest], wbuf.at[:, theirs, k_rest], sib_sem, sibling).wait_recv()

    def product(tap, group):
        out = None
        for k in range(2):
            span = pl.ds(pl.multiple_of(768 * k + 384 * group, 128), 384)
            term = jnp.dot(wbuf[tap, :, span], act[span, :], preferred_element_type=F32)
            out = term if out is None else out + term
        return out

    group = y // 4

    def early(tap, carry):
        taps[tap] = product(tap, group)
        return carry

    lax.fori_loop(0, TAPS, early, 0)

    for piece in range(2):
        step(0, 4, piece)
    activate(0, behind(4))
    for piece in range(2):
        step(1, 4, piece)
    activate(1, ahead(4))

    for tap in range(TAPS):
        full = taps[tap] + product(tap, 1 - group)
        delta = STEP * (tap - 2)
        if delta != 0:
            full = pltpu.roll(full, (-delta) % EXT, 1)
        full = full[:, 0:SEG]
        if tap == 0:
            acc[...] = full
        else:
            acc[...] += full

    tables[2].wait()

    for t in range(4):
        cols = slice(128 * t, 128 * t + 128)
        own_cols = pl.ds(pl.multiple_of(SEG * x + 128 * t, 128), 128)
        tv[mine, cols] = (
            xv[:, own_cols].astype(F32) + acc[mine, cols] + bcol[mine, :]
        ).astype(BF16)
        tv[theirs, cols] = (
            raw_b[y, 0:OWN, cols].astype(F32) + acc[theirs, cols] + bcol[theirs, :]
        ).astype(BF16)
    copy_t = go(send(tv.at[theirs, :], tout_hbm.at[:, half], tout_sem, partner))
    store_t = pltpu.make_async_copy(tv.at[mine, :], tout_hbm.at[:, half], local_sem.at[4])
    store_t.start()
    pooled = jnp.dot(tv[...], pool[...], preferred_element_type=F32).astype(BF16)
    zpool[pl.ds(pl.multiple_of(OWN * y, 32), OWN), :] = pooled[0:OWN]
    zpool[pl.ds(pl.multiple_of(768 + OWN * y, 32), OWN), :] = pooled[OWN:]
    pooled_f = pooled.astype(F32)
    squares = jnp.sum(pooled_f * pooled_f, axis=0, keepdims=True)
    proj = jnp.dot(pp_ref[...], zpool[...], preferred_element_type=F32)
    lane16 = lax.broadcasted_iota(jnp.int32, (16, 128), 1) // 32
    folded = proj[0:16]
    for q in range(1, 4):
        folded = jnp.where(lane16 == q, proj[16 * q : 16 * q + 16], folded)
    squares = jnp.broadcast_to(squares, (8, 128))
    rest = squares - squares.astype(BF16).astype(F32)
    part[y] = jnp.concatenate([folded, squares, rest], axis=0).astype(BF16)
    for j in range(1, NY):
        go(send(part.at[y], part.at[y], part_sem.at[j], ypeer[j]))
    whole = part[y].astype(F32)
    for j in range(1, NY):
        frm = (y + NY - j) % NY
        send(part.at[y], part.at[frm], part_sem.at[j], ypeer[j]).wait_recv()
        whole = whole + part[frm].astype(F32)
    norm = lax.rsqrt((whole[16:17] + whole[24:25]) * (1.0 / CH) + EPSILON)
    sides = (whole[0:16] * norm).astype(BF16)
    side[x] = sides
    copy_side = go(send(side.at[x], side.at[x], side_sem.at[0], partner))
    copy_c = send(side.at[x], side.at[2], side_sem.at[1], dest)

    @pl.when(jnp.logical_not(to_self))
    def _():
        copy_c.start()

    @pl.when(jnp.logical_not(to_self))
    def _():
        copy_c.wait_recv()

    @pl.when(to_self)
    def _():
        side[2] = side[x]

    copy_side.wait_recv()
    store_s = pltpu.make_async_copy(side, sides_hbm, local_sem.at[9])
    store_s.start()

    store_wide.wait()
    store_t.wait()
    send(tv.at[theirs, :], tout_hbm.at[:, other_half], tout_sem, partner).wait_recv()
    for copy in sent:
        copy.wait_send()
    edge_up.wait_send()
    edge_down.wait_send()

    @pl.when(jnp.logical_not(to_self))
    def _():
        copy_c.wait_send()

    store_s.wait()


def pair_kernel(
    trunk_hbm, sides_hbm, wide_hbm, pair_hbm, pb_hbm, tout_hbm, pout_hbm,
    side, wide, pin, pov, pb, mix, rows_t, sem, in_sem, out_sem,
):
    loads = [
        pltpu.make_async_copy(src, dst, sem.at[k])
        for k, (src, dst) in enumerate(((sides_hbm, side), (wide_hbm, wide), (pb_hbm, pb)))
    ]
    for copy in loads:
        copy.start()
    for b in range(4):
        span = pl.ds(16 * b, 16)
        pltpu.make_async_copy(pair_hbm.at[span], pin.at[span], in_sem.at[b]).start()
    copy_t = pltpu.make_async_copy(trunk_hbm, tout_hbm, sem.at[3])
    copy_t.start()
    v_of = lax.broadcasted_iota(jnp.int32, (32, 256), 0)
    column = lax.broadcasted_iota(jnp.int32, (32, 256), 1)
    spread = jnp.where(column // 8 == v_of, 1.0, 0.0).astype(BF16)
    loads[0].wait()
    s0 = side[0].astype(F32)
    s1 = side[1].astype(F32)
    cs = side[2].astype(F32)
    low = lax.broadcasted_iota(jnp.int32, (16, 128), 1) < 32
    row_t = jnp.concatenate(
        [
            jnp.where(low, s0, pltpu.roll(s1, 32, 1)),
            jnp.where(low, pltpu.roll(s0, 96, 1), s1),
        ],
        axis=0,
    )
    row_side = jnp.transpose(row_t)[0:64].astype(BF16)
    col_t = jnp.concatenate([pltpu.roll(cs, 64, 1), pltpu.roll(cs, 32, 1)], axis=0)
    col_side = jnp.transpose(col_t)[0:32].astype(BF16)
    repeated = jnp.dot(col_side, spread, preferred_element_type=F32)
    for i in range(8):
        mix[32 * i : 32 * i + 32, :] = jnp.where(column % 8 == i, repeated, 0.0).astype(BF16)
    loads[1].wait()
    rows_t[...] = jnp.dot(row_side, wide[...], preferred_element_type=F32)
    loads[2].wait()
    for g in range(8):
        if g % 2 == 0:
            span = pl.ds(8 * g, 16)
            pltpu.make_async_copy(pair_hbm.at[span], pin.at[span], in_sem.at[g // 2]).wait()
        stack = jnp.concatenate(
            [rows_t[8 * g : 8 * g + 8, 128 * v : 128 * v + 128] for v in range(32)], axis=0
        ).astype(BF16)
        update = jnp.dot(mix[...], stack, preferred_element_type=F32).reshape(8, 32, 128)
        span = slice(8 * g, 8 * g + 8)
        pov[span] = (pin[span].astype(F32) + update + pb[...].reshape(1, 1, 128)).astype(BF16)
        span = pl.ds(8 * g, 8)
        pltpu.make_async_copy(pov.at[span], pout_hbm.at[span], out_sem.at[g]).start()
    for g in range(8):
        span = pl.ds(8 * g, 8)
        pltpu.make_async_copy(pov.at[span], pout_hbm.at[span], out_sem.at[g]).wait()
    copy_t.wait()


VMEM_LIMIT = 60 * 1024 * 1024


def per_device(trunk_in, conv_weight, conv_bias, norm_gain, pair_proj, pair_in, opm_weight, pair_bias):
    hbm = pl.BlockSpec(memory_space=pltpu.HBM)
    dma = pltpu.SemaphoreType.DMA
    trunk, sides, wide = pl.pallas_call(
        kernel,
        name="trunk",
        out_shape=(
            jax.ShapeDtypeStruct(trunk_in.shape, BF16),
            jax.ShapeDtypeStruct((3, 16, 128), BF16),
            jax.ShapeDtypeStruct((32, 4096), BF16),
        ),
        in_specs=[hbm] * 6,
        out_specs=(hbm, hbm, hbm),
        scratch_shapes=[
            pltpu.VMEM((OWN, 1024), BF16),
            pltpu.VMEM((TAPS, 2 * OWN, CH), BF16),
            pltpu.VMEM((NY, OWN, SEG), BF16),
            pltpu.VMEM((NY, OWN, SEG), BF16),
            pltpu.VMEM((OWN, EXT), BF16),
            pltpu.VMEM((2, OWN, 128), BF16),
            pltpu.VMEM((NY, 64, 128), BF16),
            pltpu.VMEM((2, 8, 128), F32),
            pltpu.VMEM((CH, EXT), BF16),
            pltpu.VMEM((CH, 128), F32),
            pltpu.VMEM((8, 128), F32),
            pltpu.VMEM((TAPS, 2 * OWN, EXT), F32),
            pltpu.VMEM((2 * OWN, SEG), F32),
            pltpu.VMEM((2 * OWN, 128), F32),
            pltpu.VMEM((2 * OWN, SEG), BF16),
            pltpu.VMEM((SEG, 128), BF16),
            pltpu.VMEM((CH, 128), BF16),
            pltpu.VMEM((NY, 32, 128), BF16),
            pltpu.VMEM((3, 16, 128), BF16),
            pltpu.VMEM((1, OWN), F32),
            pltpu.VMEM((12, 128), F32),
            pltpu.VMEM((64, CH), BF16),
            pltpu.VMEM((1024, 128), BF16),
            pltpu.VMEM((1024, 128), F32),
            pltpu.VMEM((32, 4096), BF16),
            dma((10,)),
            dma((2,)),
            dma((2,)),
            dma((4, 2)),
            dma((2, 2, 4, 2, 2)),
            dma((NY, 2)),
            dma((2, 2)),
            dma((2,)),
            dma((2,)),
            dma((NY, 2)),
            dma((2, 2)),
        ],
        compiler_params=pltpu.CompilerParams(
            collective_id=0, has_side_effects=True, vmem_limit_bytes=VMEM_LIMIT
        ),
        cost_estimate=pl.CostEstimate(
            flops=1_600_000_000, bytes_accessed=3_000_000, transcendentals=1_000_000
        ),
    )(
        trunk_in, conv_weight, conv_bias.reshape(1, OWN), norm_gain.reshape(12, 128), pair_proj,
        opm_weight,
    )
    return pl.pallas_call(
        pair_kernel,
        name="pair",
        out_shape=(
            jax.ShapeDtypeStruct(trunk_in.shape, BF16),
            jax.ShapeDtypeStruct(pair_in.shape, BF16),
        ),
        in_specs=[hbm] * 5,
        out_specs=(hbm, hbm),
        scratch_shapes=[
            pltpu.VMEM((3, 16, 128), BF16),
            pltpu.VMEM((32, 4096), BF16),
            pltpu.VMEM((64, 32, 128), BF16),
            pltpu.VMEM((64, 32, 128), BF16),
            pltpu.VMEM((1, 128), F32),
            pltpu.VMEM((256, 256), BF16),
            pltpu.VMEM((64, 4096), F32),
            dma((4,)),
            dma((4,)),
            dma((8,)),
        ],
        compiler_params=pltpu.CompilerParams(vmem_limit_bytes=VMEM_LIMIT),
        cost_estimate=pl.CostEstimate(flops=200_000_000, bytes_accessed=2_000_000, transcendentals=0),
    )(trunk, sides, wide, pair_in, pair_bias.reshape(1, 128))


def solution(mesh):
    return jax.shard_map(
        per_device,
        mesh=mesh,
        in_specs=(
            P("col", "row"), P(None, "col", None), P("col"), P(), P(), P("row", "col", None), P(), P(),
        ),
        out_specs=(P("col", "row"), P("row", "col", None)),
        check_vma=False,
    )
```

time: 63.1 us -> 55.9 us (0.89)
  local copies, waits for them, and re-layouts: 8.7 us -> 0 us
  Pallas kernels: 53 us -> 54.5 us
    unnamed x16 -> x0, local copies, waits for them, and re-layouts: 8.04 us -> none
    pallas_call x1 -> x2, Pallas kernels: 53 us -> 54.5 us  [the longest x1 47.3 us: per_device(): pl.pallas_call(kernel, name='trunk', out_shape=(jax.ShapeDtypeStruct(trun...]
    reshape x1 -> x0, local copies, waits for them, and re-layouts: 0.66 us -> none  [per_device(): bias_row = jnp.pad(conv_bias, (0, 128 - OWN)).reshape(1, 128)]
where the time goes in v2:
time: 55.9 us; the launch traced here: 55.2 us
  Pallas kernels  54.5 us (97%)
  between operations  0.64 us (1%)
    pallas_call x1, Pallas kernels, per_device(): pl.pallas_call(kernel, name='trunk', out_shape=(jax.ShapeDtypeStruct(trun...  47.3 us
    pallas_call x1, Pallas kernels, per_device(): pl.pallas_call(pair_kernel, name='pair', out_shape=(jax.ShapeDtypeStruct(...  7.21 us

profile of v2, /device:TPU:1, one launch (start us, length us, event | category | flops | bytes accessed | tf_op | source)
XLA Modules:
  0.0 55.2 jit_solution(3243459543953401393)
XLA Ops:
  0.6 47.3 %trunk.1 = (bf16[96,1024]{1,0:T(8,128)(2,1)}, bf16[3,16,128]{2,1,0:T(8,128)(2,1)}, bf16[32,4096]{1,0:T(8,128)(2,1)}) custom-call(bf16[96,1024]{1,0:T(8,128)(2,1)} %x_hbm.1, bf16[5,96,1536]{2,1,0:T(8,128)(2,1)} %w_hbm.1, f32[1,96]{1,0:T(1,128)} %bitcast.5, f32[12,128]{1,0:T(8,128)} %bitcast.4, bf16[64,1536]{1,0:T(8,128)(2,1)} %pp_hbm.1, bf16[1024,128]{1,0:T(8,128)(2,1)} %opm_hbm.1), custom_call_target="tpu_custom_call" | custom-call | flops 1600000000 | bytes 3000000 | tf_op jit(solution)/shard_map/trunk/pallas_call | solution.py:473
  48.0 7.2 %pair.1 = (bf16[96,1024]{1,0:T(8,128)(2,1)}, bf16[64,32,128]{2,1,0:T(8,128)(2,1)}) custom-call(bf16[96,1024]{1,0:T(8,128)(2,1)} %get-tuple-element.5.trunk_hbm, bf16[3,16,128]{2,1,0:T(8,128)(2,1)} %get-tuple-element.6.sides_hbm, bf16[32,4096]{1,0:T(8,128)(2,1)} %get-tuple-element.7.wide_hbm, bf16[64,32,128]{2,1,0:T(8,128)(2,1)} %pair_hbm.1, f32[1,128]{1,0:T(1,128)} %bitcast.3), custom_call_target="tpu_custom_call" | custom-call | flops 200000000 | bytes 2000000 | tf_op jit(solution)/shard_map/pair/pallas_call | solution.py:531

commit v3 on v2

--- a/solution.py
+++ b/solution.py
@@ -22,17 +22,18 @@
 
 
 def gelu(v):
-    u = 0.7978845608028654 * (v + 0.044715 * (v * v * v))
-    return (0.5 * v) * (1.0 + jnp.tanh(u))
+    u = v * (0.7978845608028654 + 0.035677408136300125 * (v * v))
+    h = 0.5 * v
+    return h + h * jnp.tanh(u)
 
 
 def kernel(
     x_hbm, w_hbm, cb_hbm, g_hbm, pp_hbm, opm_hbm,
-    tout_hbm, sides_hbm, wide_hbm,
-    xv, wbuf, raw_a, raw_b, swap, edge, hal, cbuf, act, gain, sc, taps, acc, bcol,
-    tv, pool, zpool, part, side, cb_ref, g_ref, pp_ref, opm_ref, opm_f, wide,
+    tout_hbm, sides_out, wide_hbm,
+    xv, wbuf, raw_a, raw_b, inner, edge, hal, stat, cbuf, act, gain, sc, taps, acc, bcol,
+    tv, pool, own_pp, part, side, cb_ref, g_ref, pp_ref, opm_ref, opm_f, wide,
     local_sem,
-    swap_sem, cb_sem, edge_sem, ring_sem, hal_sem, w_sem, sib_sem, tout_sem, part_sem, side_sem,
+    swap_sem, inner_sem, cb_sem, edge_sem, ring_sem, hal_sem, stat_sem, w_sem, sib_sem, tout_sem, part_sem, side_sem,
 ):
     r = lax.axis_index("row")
     c = lax.axis_index("col")
@@ -75,8 +76,7 @@
         copy.start()
 
     barrier = pltpu.get_barrier_semaphore()
-    diagonal = [(r, (1 - x) * NY + (y + j) % NY) for j in (1, NY - 1)]
-    greet = [partner, across, sibling] + diagonal + ypeer[1:] + [(my_edge, y), (my_edge, NY + y)]
+    greet = [partner, across, sibling] + ypeer[1:] + [(my_edge, y), (my_edge, NY + y)]
     for dev in greet:
         pl.semaphore_signal(barrier, inc=1, device_id=dev, device_id_type=MESH)
 
@@ -105,11 +105,7 @@
         owner = (y + NY - (dist - 1)) % NY if direction == 0 else (y + dist - 1) % NY
         at = piece_of(kind, owner, piece)
         dev = ypeer[1] if direction == 0 else ypeer[NY - 1]
-        src = at
-        if kind == 1 and dist == 1:
-            src = xv.at[48 * piece : 48 * piece + 48, other_half]
-            dev = diagonal[direction]
-        return send(src, at, ring_sem.at[direction, kind, dist - 1, piece], dev)
+        return send(at, at, ring_sem.at[direction, kind, dist - 1, piece], dev)
 
     def arrived(direction, kind, dist, piece):
         owner = (y + NY - dist) % NY if direction == 0 else (y + dist) % NY
@@ -126,7 +122,19 @@
             if dist < 3 or (dist == 3 and kind == 1):
                 go(ring(1, kind, dist + 1, piece))
 
-    other_half = pl.ds(pl.multiple_of(SEG * (1 - x), 128), SEG)
+    def halo_ring(direction, dist):
+        owner = (y + NY - (dist - 1)) % NY if direction == 0 else (y + dist - 1) % NY
+        dev = ypeer[1] if direction == 0 else ypeer[NY - 1]
+        return send(hal.at[owner], hal.at[owner], hal_sem.at[direction, dist - 1], dev)
+
+    def halo_step(dist):
+        for direction in range(2 if dist < 4 else 1):
+            owner = (y + NY - dist) % NY if direction == 0 else (y + dist) % NY
+            at = hal.at[owner]
+            send(at, at, hal_sem.at[direction, dist - 1], ypeer[1]).wait_recv()
+            if dist < 3 or (dist == 3 and direction == 0):
+                go(halo_ring(direction, dist + 1))
+
     other = 1 - x
     edge_up = send(xv.at[:, 896:1024], edge.at[x], edge_sem.at[x], (up, y))
     edge_down = send(xv.at[:, 0:128], edge.at[x], edge_sem.at[2 + x], (down, NY + y))
@@ -135,12 +143,16 @@
     for piece in range(2):
         for direction in range(2):
             go(ring(direction, 0, 1, piece))
-    copy_swap = go(send(
-        xv.at[:, pl.ds(pl.multiple_of(384 * other, 128), EXT)], swap, swap_sem, partner
+    other_half = pl.ds(pl.multiple_of(SEG * other, 128), SEG)
+    copy_swap = [
+        go(send(
+            xv.at[48 * p : 48 * p + 48, other_half], piece_of(1, y, p), swap_sem.at[p], partner
+        ))
+        for p in range(2)
+    ]
+    copy_inner = go(send(
+        xv.at[:, pl.ds(pl.multiple_of(SEG - 128 * other, 128), 128)], inner, inner_sem, partner
     ))
-    for piece in range(2):
-        for direction in range(2):
-            go(ring(direction, 1, 1, piece))
     copy_cb = go(send(cbuf.at[x], cbuf.at[x], cb_sem, partner))
     quarters = [pl.ds(pl.multiple_of(768 * core + 384 * q, 128), 384) for q in range(2)]
     mine = pl.ds(pl.multiple_of(OWN * x, 32), OWN)
@@ -158,8 +170,12 @@
         )
     for piece in range(2):
         step(0, 1, piece)
-
-    copy_swap.wait_recv()
+    for piece in range(2):
+        copy_swap[piece].wait_recv()
+        go(ring(0, 1, 1, piece))
+        go(ring(1, 1, 1, piece))
+
+    copy_inner.wait_recv()
     for k in range(2):
 
         @pl.when(x == 0)
@@ -170,9 +186,8 @@
         def _():
             send(xv.at[:, 0:128], edge.at[k], edge_sem.at[2 + k], (up, y)).wait_recv()
 
-    raw_b[y, 0:OWN, :] = swap[:, pl.ds(pl.multiple_of(128 * x, 128), SEG)]
     own_f = xv[:, half].astype(F32)
-    their_f = raw_b[y, 0:OWN, :].astype(F32)
+    their_f = raw_b[y].astype(F32)
     sums = jnp.sum(own_f * own_f + their_f * their_f, axis=0, keepdims=True)
     at_end = jnp.logical_or(
         jnp.logical_and(x == 0, r == 0), jnp.logical_and(x == 1, r == NROW - 1)
@@ -180,34 +195,44 @@
     lane = lax.broadcasted_iota(jnp.int32, (OWN, 128), 1)
     pick_inner = (lane < 64) == (x == 0)
     inner_a = xv[:, pl.ds(pl.multiple_of(SEG - 128 * x, 128), 128)].astype(F32)
-    inner_b = swap[:, pl.ds(pl.multiple_of(SEG * other, 128), 128)].astype(F32)
+    inner_b = inner[...].astype(F32)
     keep = jnp.where(at_end, 0.0, 1.0)
     outer_a = edge[x].astype(F32) * keep
     outer_b = edge[other].astype(F32) * keep
     halo_a = jnp.where(pick_inner, inner_a, outer_a)
     halo_b = jnp.where(pick_inner, inner_b, outer_b)
     halo_sums = jnp.sum(halo_a * halo_a + halo_b * halo_b, axis=0, keepdims=True)
+    sums = jnp.concatenate(
+        [sums[:, 128 * t : 128 * t + 128] for t in range(4)]
+        + [halo_sums, jnp.zeros((3, 128), F32)],
+        axis=0,
+    )
+    rest = sums - sums.astype(BF16).astype(F32)
+    stat[y] = jnp.concatenate([sums, rest], axis=0).astype(BF16)
+    for j in range(1, NY):
+        go(send(stat.at[y], stat.at[y], stat_sem.at[j], ypeer[j]))
     lane48 = lax.broadcasted_iota(jnp.int32, (48, 128), 1)
     packed = halo_a[0:48]
     for q, piece in ((1, halo_a[48:96]), (2, halo_b[0:48]), (3, halo_b[48:96])):
         moved = pltpu.roll(piece, 32 * q, 1)
         inside = jnp.logical_and(lane48 >= 32 * q - 16, lane48 < 32 * q + 16)
         packed = jnp.where(inside, moved, packed)
-    sums = jnp.concatenate(
-        [sums[:, 128 * t : 128 * t + 128] for t in range(4)]
-        + [halo_sums, jnp.zeros((3, 128), F32)],
-        axis=0,
-    )
-    rest = sums - sums.astype(BF16).astype(F32)
-    hal[y] = jnp.concatenate([packed, sums, rest], axis=0).astype(BF16)
-    for j in range(1, NY):
-        go(send(hal.at[y], hal.at[y], hal_sem.at[j], ypeer[j]))
+    hal[y] = packed.astype(BF16)
+    go(halo_ring(0, 1))
+    go(halo_ring(1, 1))
+    for piece in range(2):
+        step(0, 2, piece)
     for piece in range(2):
         step(1, 1, piece)
     token = lax.broadcasted_iota(jnp.int32, (SEG, 128), 0) // 16
     cell = lax.broadcasted_iota(jnp.int32, (SEG, 128), 1) % 32
     pool[...] = jnp.where(token == cell, 0.0625, 0.0).astype(BF16)
-    zpool[...] = jnp.zeros(zpool.shape, BF16)
+    tables[2].wait()
+    channel = lax.broadcasted_iota(jnp.int32, (CH, 2 * OWN), 0)
+    place = lax.broadcasted_iota(jnp.int32, (CH, 2 * OWN), 1)
+    wanted = place + OWN * y + jnp.where(place >= OWN, 768 - OWN, 0)
+    choose = jnp.where(channel == wanted, 1.0, 0.0).astype(BF16)
+    own_pp[...] = jnp.dot(pp_ref[...], choose, preferred_element_type=F32).astype(BF16)
     tables[3].wait()
     opm_f[...] = opm_ref[...].astype(F32)
     for v in range(32):
@@ -220,17 +245,16 @@
             jnp.broadcast_to(cbuf[k, 0:1, :], (128, 128))
         )[0:OWN]
 
-    for piece in range(2):
-        step(0, 2, piece)
+    halo_step(1)
 
     def sums_of(owner):
-        both = hal[owner, 48:64, :].astype(F32)
+        both = stat[owner].astype(F32)
         return both[0:8] + both[8:16]
 
     total = sums_of(y)
     for j in range(1, NY):
         frm = (y + NY - j) % NY
-        send(hal.at[y], hal.at[frm], hal_sem.at[j], ypeer[j]).wait_recv()
+        send(stat.at[y], stat.at[frm], stat_sem.at[j], ypeer[j]).wait_recv()
         total = total + sums_of(frm)
     sc[...] = lax.rsqrt(total * (1.0 / CH) + EPSILON)
 
@@ -241,20 +265,16 @@
         buf = (raw_a, raw_b)[kind]
         base = first_row(kind, owner)
 
-        def body(b, carry):
-            rows = pl.ds(pl.multiple_of(b * 32, 32), 32)
-            target = pl.ds(pl.multiple_of(base + b * 32, 32), 32)
+        for b in range(0, OWN, 16):
+            target = pl.ds(pl.multiple_of(base + b, 16), 16)
             g = gain[target, :]
             for t in range(4):
                 cols = slice(128 * t, 128 * t + 128)
-                v = buf[owner, rows, cols].astype(F32) * g * sc[t : t + 1, :]
+                v = buf[owner, b : b + 16, cols].astype(F32) * g * sc[t : t + 1, :]
                 act[target, cols] = gelu(v).astype(BF16)
-            return carry
-
-        lax.fori_loop(0, 3, body, 0)
 
     def activate_halo(owner):
-        block = hal[owner, 0:48, :].astype(F32)
+        block = hal[owner].astype(F32)
         for q in range(4):
             piece = block if q == 0 else pltpu.roll(block, 128 - 32 * q, 1)
             base = first_row(q // 2, owner) + 48 * (q % 2)
@@ -268,22 +288,23 @@
     def ahead(d):
         return (y + d) % NY
 
+    for piece in range(2):
+        step(0, 3, piece)
     activate(0, y)
     activate(1, y)
     for piece in range(2):
         step(1, 2, piece)
+    halo_step(2)
     activate_halo(y)
     for owner in (behind(1), ahead(1)):
         activate(0, owner)
         activate(1, owner)
-    for piece in range(2):
-        step(0, 3, piece)
-    for owner in (behind(1), ahead(1)):
         activate_halo(owner)
     for owner in (behind(2), ahead(2)):
         activate(0, owner)
     for piece in range(2):
         step(1, 3, piece)
+    halo_step(3)
     for q in range(2):
         send(
             w_hbm.at[:, :, quarters[q]], wbuf.at[:, theirs, quarters[q]], w_sem.at[q], partner
@@ -298,7 +319,6 @@
         activate(0, owner)
         activate(1, owner)
         activate_halo(owner)
-    activate_halo(ahead(4))
     load_w.wait()
     send(wbuf.at[:, theirs, k_rest], wbuf.at[:, theirs, k_rest], sib_sem, sibling).wait_recv()
 
@@ -321,6 +341,8 @@
     for piece in range(2):
         step(0, 4, piece)
     activate(0, behind(4))
+    halo_step(4)
+    activate_halo(behind(4))
     for piece in range(2):
         step(1, 4, piece)
     activate(1, ahead(4))
@@ -336,8 +358,6 @@
         else:
             acc[...] += full
 
-    tables[2].wait()
-
     for t in range(4):
         cols = slice(128 * t, 128 * t + 128)
         own_cols = pl.ds(pl.multiple_of(SEG * x + 128 * t, 128), 128)
@@ -345,17 +365,12 @@
             xv[:, own_cols].astype(F32) + acc[mine, cols] + bcol[mine, :]
         ).astype(BF16)
         tv[theirs, cols] = (
-            raw_b[y, 0:OWN, cols].astype(F32) + acc[theirs, cols] + bcol[theirs, :]
+            raw_b[y, :, cols].astype(F32) + acc[theirs, cols] + bcol[theirs, :]
         ).astype(BF16)
-    copy_t = go(send(tv.at[theirs, :], tout_hbm.at[:, half], tout_sem, partner))
-    store_t = pltpu.make_async_copy(tv.at[mine, :], tout_hbm.at[:, half], local_sem.at[4])
-    store_t.start()
     pooled = jnp.dot(tv[...], pool[...], preferred_element_type=F32).astype(BF16)
-    zpool[pl.ds(pl.multiple_of(OWN * y, 32), OWN), :] = pooled[0:OWN]
-    zpool[pl.ds(pl.multiple_of(768 + OWN * y, 32), OWN), :] = pooled[OWN:]
     pooled_f = pooled.astype(F32)
     squares = jnp.sum(pooled_f * pooled_f, axis=0, keepdims=True)
-    proj = jnp.dot(pp_ref[...], zpool[...], preferred_element_type=F32)
+    proj = jnp.dot(own_pp[...], pooled, preferred_element_type=F32)
     lane16 = lax.broadcasted_iota(jnp.int32, (16, 128), 1) // 32
     folded = proj[0:16]
     for q in range(1, 4):
@@ -365,6 +380,9 @@
     part[y] = jnp.concatenate([folded, squares, rest], axis=0).astype(BF16)
     for j in range(1, NY):
         go(send(part.at[y], part.at[y], part_sem.at[j], ypeer[j]))
+    copy_t = go(send(tv.at[theirs, :], tout_hbm.at[:, half], tout_sem, partner))
+    store_t = pltpu.make_async_copy(tv.at[mine, :], tout_hbm.at[:, half], local_sem.at[4])
+    store_t.start()
     whole = part[y].astype(F32)
     for j in range(1, NY):
         frm = (y + NY - j) % NY
@@ -389,8 +407,7 @@
         side[2] = side[x]
 
     copy_side.wait_recv()
-    store_s = pltpu.make_async_copy(side, sides_hbm, local_sem.at[9])
-    store_s.start()
+    sides_out[...] = side[...]
 
     store_wide.wait()
     store_t.wait()
@@ -404,28 +421,25 @@
     def _():
         copy_c.wait_send()
 
-    store_s.wait()
-
 
 def pair_kernel(
-    trunk_hbm, sides_hbm, wide_hbm, pair_hbm, pb_hbm, tout_hbm, pout_hbm,
-    side, wide, pin, pov, pb, mix, rows_t, sem, in_sem, out_sem,
+    trunk_hbm, side, wide_hbm, pair_hbm, pb_hbm, tout_hbm, pout_hbm,
+    wide, pin, pov, pb, mix, rows_t, trunk, sem, in_sem, out_sem,
 ):
     loads = [
         pltpu.make_async_copy(src, dst, sem.at[k])
-        for k, (src, dst) in enumerate(((sides_hbm, side), (wide_hbm, wide), (pb_hbm, pb)))
+        for k, (src, dst) in enumerate(((wide_hbm, wide), (pb_hbm, pb)))
     ]
     for copy in loads:
         copy.start()
     for b in range(4):
         span = pl.ds(16 * b, 16)
         pltpu.make_async_copy(pair_hbm.at[span], pin.at[span], in_sem.at[b]).start()
-    copy_t = pltpu.make_async_copy(trunk_hbm, tout_hbm, sem.at[3])
-    copy_t.start()
+    load_t = pltpu.make_async_copy(trunk_hbm, trunk, sem.at[3])
+    load_t.start()
     v_of = lax.broadcasted_iota(jnp.int32, (32, 256), 0)
     column = lax.broadcasted_iota(jnp.int32, (32, 256), 1)
     spread = jnp.where(column // 8 == v_of, 1.0, 0.0).astype(BF16)
-    loads[0].wait()
     s0 = side[0].astype(F32)
     s1 = side[1].astype(F32)
     cs = side[2].astype(F32)
@@ -443,9 +457,12 @@
     repeated = jnp.dot(col_side, spread, preferred_element_type=F32)
     for i in range(8):
         mix[32 * i : 32 * i + 32, :] = jnp.where(column % 8 == i, repeated, 0.0).astype(BF16)
+    load_t.wait()
+    copy_t = pltpu.make_async_copy(trunk, tout_hbm, sem.at[4])
+    copy_t.start()
+    loads[0].wait()
+    rows_t[...] = jnp.dot(row_side, wide[...], preferred_element_type=F32)
     loads[1].wait()
-    rows_t[...] = jnp.dot(row_side, wide[...], preferred_element_type=F32)
-    loads[2].wait()
     for g in range(8):
         if g % 2 == 0:
             span = pl.ds(8 * g, 16)
@@ -479,15 +496,16 @@
             jax.ShapeDtypeStruct((32, 4096), BF16),
         ),
         in_specs=[hbm] * 6,
-        out_specs=(hbm, hbm, hbm),
+        out_specs=(hbm, pl.BlockSpec(memory_space=pltpu.VMEM), hbm),
         scratch_shapes=[
             pltpu.VMEM((OWN, 1024), BF16),
             pltpu.VMEM((TAPS, 2 * OWN, CH), BF16),
             pltpu.VMEM((NY, OWN, SEG), BF16),
             pltpu.VMEM((NY, OWN, SEG), BF16),
-            pltpu.VMEM((OWN, EXT), BF16),
+            pltpu.VMEM((OWN, 128), BF16),
             pltpu.VMEM((2, OWN, 128), BF16),
-            pltpu.VMEM((NY, 64, 128), BF16),
+            pltpu.VMEM((NY, 48, 128), BF16),
+            pltpu.VMEM((NY, 16, 128), BF16),
             pltpu.VMEM((2, 8, 128), F32),
             pltpu.VMEM((CH, EXT), BF16),
             pltpu.VMEM((CH, 128), F32),
@@ -497,7 +515,7 @@
             pltpu.VMEM((2 * OWN, 128), F32),
             pltpu.VMEM((2 * OWN, SEG), BF16),
             pltpu.VMEM((SEG, 128), BF16),
-            pltpu.VMEM((CH, 128), BF16),
+            pltpu.VMEM((64, 2 * OWN), BF16),
             pltpu.VMEM((NY, 32, 128), BF16),
             pltpu.VMEM((3, 16, 128), BF16),
             pltpu.VMEM((1, OWN), F32),
@@ -507,10 +525,12 @@
             pltpu.VMEM((1024, 128), F32),
             pltpu.VMEM((32, 4096), BF16),
             dma((10,)),
+            dma((2, 2)),
             dma((2,)),
             dma((2,)),
             dma((4, 2)),
             dma((2, 2, 4, 2, 2)),
+            dma((2, 4, 2)),
             dma((NY, 2)),
             dma((2, 2)),
             dma((2,)),
@@ -535,17 +555,17 @@
             jax.ShapeDtypeStruct(trunk_in.shape, BF16),
             jax.ShapeDtypeStruct(pair_in.shape, BF16),
         ),
-        in_specs=[hbm] * 5,
+        in_specs=[hbm, pl.BlockSpec(memory_space=pltpu.VMEM), hbm, hbm, hbm],
         out_specs=(hbm, hbm),
         scratch_shapes=[
-            pltpu.VMEM((3, 16, 128), BF16),
             pltpu.VMEM((32, 4096), BF16),
             pltpu.VMEM((64, 32, 128), BF16),
             pltpu.VMEM((64, 32, 128), BF16),
             pltpu.VMEM((1, 128), F32),
             pltpu.VMEM((256, 256), BF16),
             pltpu.VMEM((64, 4096), F32),
-            dma((4,)),
+            pltpu.VMEM((OWN, 1024), BF16),
+            dma((5,)),
             dma((4,)),
             dma((8,)),
         ],

time: 55.9 us -> 52.9 us (0.946)
  the two profiles are of different devices: /device:TPU:1 before, /device:TPU:64 now
where the time goes in v3:
time: 52.9 us; the launch traced here: 52.7 us
  Pallas kernels  52 us (98%)
  between operations  0.64 us (1%)
    pallas_call x1, Pallas kernels, per_device(): pl.pallas_call(kernel, name='trunk', out_shape=(jax.ShapeDtypeStruct(trun...  48.2 us
    pallas_call x1, Pallas kernels, per_device(): pl.pallas_call(pair_kernel, name='pair', out_shape=(jax.ShapeDtypeStruct(...  3.86 us

profile of v3, /device:TPU:64, one launch (start us, length us, event | category | flops | bytes accessed | tf_op | source)
XLA Modules:
  0.0 52.7 jit_solution(8333904878979311615)
XLA Ops:
  0.6 48.2 %trunk.1 = (bf16[96,1024]{1,0:T(8,128)(2,1)}, bf16[3,16,128]{2,1,0:T(8,128)(2,1)}, bf16[32,4096]{1,0:T(8,128)(2,1)}) custom-call(bf16[96,1024]{1,0:T(8,128)(2,1)} %x_hbm.1, bf16[5,96,1536]{2,1,0:T(8,128)(2,1)} %w_hbm.1, f32[1,96]{1,0:T(1,128)} %bitcast.5, f32[12,128]{1,0:T(8,128)} %bitcast.4, bf16[64,1536]{1,0:T(8,128)(2,1)} %pp_hbm.1, bf16[1024,128]{1,0:T(8,128)(2,1)} %opm_hbm.1), custom_call_target="tpu_custom_call" | custom-call | flops 1600000000 | bytes 3000000 | tf_op jit(solution)/shard_map/trunk/pallas_call | solution.py:490
  48.8 3.9 %pair.1 = (bf16[96,1024]{1,0:T(8,128)(2,1)}, bf16[64,32,128]{2,1,0:T(8,128)(2,1)}) custom-call(bf16[96,1024]{1,0:T(8,128)(2,1)} %get-tuple-element.5.trunk_hbm, bf16[3,16,128]{2,1,0:T(8,128)(2,1)} %get-tuple-element.6.side, bf16[32,4096]{1,0:T(8,128)(2,1)} %get-tuple-element.7.wide_hbm, bf16[64,32,128]{2,1,0:T(8,128)(2,1)} %pair_hbm.1, f32[1,128]{1,0:T(1,128)} %bitcast.3), custom_call_target="tpu_custom_call" | custom-call | flops 200000000 | bytes 2000000 | tf_op jit(solution)/shard_map/pair/pallas_call | solution.py:551

commit v4 on v3

--- a/solution.py
+++ b/solution.py
@@ -29,11 +29,11 @@
 
 def kernel(
     x_hbm, w_hbm, cb_hbm, g_hbm, pp_hbm, opm_hbm,
-    tout_hbm, sides_out, wide_hbm,
+    tout_hbm, sides_hbm, wide_hbm,
     xv, wbuf, raw_a, raw_b, inner, edge, hal, stat, cbuf, act, gain, sc, taps, acc, bcol,
-    tv, pool, own_pp, part, side, cb_ref, g_ref, pp_ref, opm_ref, opm_f, wide,
+    tv, pool, own_pp, prow, pcol, mcol, side, cb_ref, g_ref, pp_ref, opm_ref, opm_f, wide,
     local_sem,
-    swap_sem, inner_sem, cb_sem, edge_sem, ring_sem, hal_sem, stat_sem, w_sem, sib_sem, tout_sem, part_sem, side_sem,
+    swap_sem, inner_sem, cb_sem, edge_sem, ring_sem, hal_sem, stat_sem, w_sem, sib_sem, tout_sem, row_sem, col_out, col_in,
 ):
     r = lax.axis_index("row")
     c = lax.axis_index("col")
@@ -46,9 +46,11 @@
     across = (r + 2 - 4 * ((r // 2) % 2), (1 - x) * NY + y)
     sibling = (r + 1 - 2 * core, c)
     ypeer = [(r, x * NY + (y + j) % NY) for j in range(NY)]
-    dest = ((r // 8) * 8 + y, 2 * (r % 8) + x)
-    source = ((r // 8) * 8 + c // 2, (c % 2) * NY + r % 8)
-    to_self = jnp.logical_and(dest[0] == r, dest[1] == c)
+    opeer = [(r, (1 - x) * NY + (y + j) % NY) for j in range(NY)]
+    window = (r // 8) * 8
+    col_dest = 2 * (r % 8) + x
+    col_source = [(window + c // 2, (c % 2) * NY + k) for k in range(NY)]
+    to_self = col_dest == c
     my_edge = r + 2 * x * 1 - 1
     my_edge = (my_edge + NROW) % NROW
 
@@ -76,20 +78,22 @@
         copy.start()
 
     barrier = pltpu.get_barrier_semaphore()
-    greet = [partner, across, sibling] + ypeer[1:] + [(my_edge, y), (my_edge, NY + y)]
+    greet = [partner, across, sibling] + ypeer[1:] + opeer[1:] + [(my_edge, y), (my_edge, NY + y)]
     for dev in greet:
         pl.semaphore_signal(barrier, inc=1, device_id=dev, device_id_type=MESH)
 
-    @pl.when(jnp.logical_not(to_self))
-    def _():
-        pl.semaphore_signal(barrier, inc=1, device_id=source, device_id_type=MESH)
+    for k in range(NY):
+
+        @pl.when(jnp.logical_not(jnp.logical_and(to_self, y == k)))
+        def _():
+            pl.semaphore_signal(barrier, inc=1, device_id=col_source[k], device_id_type=MESH)
 
     cbuf[pl.ds(x, 1)] = jnp.zeros((1, 8, 128), F32)
     tables[0].wait()
     cbuf[pl.ds(x, 1), :, 0:OWN] = jnp.broadcast_to(cb_ref[...].reshape(1, 1, OWN), (1, 8, OWN))
     load_x.wait()
     load_a.wait()
-    pl.semaphore_wait(barrier, len(greet) + jnp.where(to_self, 0, 1))
+    pl.semaphore_wait(barrier, len(greet) + NY - jnp.where(to_self, 1, 0))
 
     sent = []
 
@@ -163,11 +167,6 @@
     for copy in tables[2:]:
         copy.start()
 
-    tables[1].wait()
-    for i in range(12):
-        gain[128 * i : 128 * i + 128, :] = jnp.transpose(
-            jnp.broadcast_to(g_ref[i : i + 1, :], (128, 128))
-        )
     for piece in range(2):
         step(0, 1, piece)
     for piece in range(2):
@@ -209,7 +208,7 @@
     )
     rest = sums - sums.astype(BF16).astype(F32)
     stat[y] = jnp.concatenate([sums, rest], axis=0).astype(BF16)
-    for j in range(1, NY):
+    for j in (4, 3, 5, 2, 6, 1, 7):
         go(send(stat.at[y], stat.at[y], stat_sem.at[j], ypeer[j]))
     lane48 = lax.broadcasted_iota(jnp.int32, (48, 128), 1)
     packed = halo_a[0:48]
@@ -220,8 +219,20 @@
     hal[y] = packed.astype(BF16)
     go(halo_ring(0, 1))
     go(halo_ring(1, 1))
+
+    tables[1].wait()
+    for i in range(12):
+        gain[128 * i : 128 * i + 128, :] = jnp.transpose(
+            jnp.broadcast_to(g_ref[i : i + 1, :], (128, 128))
+        )
     for piece in range(2):
         step(0, 2, piece)
+    tables[3].wait()
+    opm_f[...] = opm_ref[...].astype(F32)
+    for v in range(32):
+        wide[:, 128 * v : 128 * v + 128] = opm_f[pl.ds(v, 32, stride=32), :].astype(BF16)
+    store_wide = pltpu.make_async_copy(wide, wide_hbm, local_sem.at[3])
+    store_wide.start()
     for piece in range(2):
         step(1, 1, piece)
     token = lax.broadcasted_iota(jnp.int32, (SEG, 128), 0) // 16
@@ -233,12 +244,6 @@
     wanted = place + OWN * y + jnp.where(place >= OWN, 768 - OWN, 0)
     choose = jnp.where(channel == wanted, 1.0, 0.0).astype(BF16)
     own_pp[...] = jnp.dot(pp_ref[...], choose, preferred_element_type=F32).astype(BF16)
-    tables[3].wait()
-    opm_f[...] = opm_ref[...].astype(F32)
-    for v in range(32):
-        wide[:, 128 * v : 128 * v + 128] = opm_f[pl.ds(v, 32, stride=32), :].astype(BF16)
-    store_wide = pltpu.make_async_copy(wide, wide_hbm, local_sem.at[3])
-    store_wide.start()
     copy_cb.wait_recv()
     for k in range(2):
         bcol[OWN * k : OWN * k + OWN, :] = jnp.transpose(
@@ -371,64 +376,101 @@
     pooled_f = pooled.astype(F32)
     squares = jnp.sum(pooled_f * pooled_f, axis=0, keepdims=True)
     proj = jnp.dot(own_pp[...], pooled, preferred_element_type=F32)
-    lane16 = lax.broadcasted_iota(jnp.int32, (16, 128), 1) // 32
-    folded = proj[0:16]
-    for q in range(1, 4):
-        folded = jnp.where(lane16 == q, proj[16 * q : 16 * q + 16], folded)
+    lane_group = lax.broadcasted_iota(jnp.int32, (8, 128), 1) // 32
     squares = jnp.broadcast_to(squares, (8, 128))
     rest = squares - squares.astype(BF16).astype(F32)
-    part[y] = jnp.concatenate([folded, squares, rest], axis=0).astype(BF16)
-    for j in range(1, NY):
-        go(send(part.at[y], part.at[y], part_sem.at[j], ypeer[j]))
+    sub = lax.broadcasted_iota(jnp.int32, (8, 128), 0)
+    squares = jnp.where(sub < 4, squares, rest)
+    folded = []
+    for first in (0, 32):
+        one = proj[first : first + 8]
+        for q in range(1, 4):
+            one = jnp.where(lane_group == q, proj[first + 8 * q : first + 8 * q + 8], one)
+        folded.append(jnp.concatenate([one, squares], axis=0).astype(BF16))
+    prow[x, y] = folded[0]
+    mcol[...] = folded[1]
+    own = prow.at[x, y]
+
+    def col_copy(k):
+        return pltpu.make_async_remote_copy(
+            src_ref=mcol, dst_ref=pcol.at[y], send_sem=col_out.at[k], recv_sem=col_in.at[y],
+            device_id=(window + k, col_dest), device_id_type=MESH,
+        )
+
+    def col_is_self(k):
+        return jnp.logical_and(to_self, r % 8 == k)
+
+    for j in (4, 3, 5, 2, 6, 1, 7):
+        go(send(own, own, row_sem.at[0, j], ypeer[j]))
+        go(send(own, own, row_sem.at[1, j], opeer[j]))
+    go(send(own, own, row_sem.at[1, 0], partner))
+    for k in range(NY):
+
+        @pl.when(jnp.logical_not(col_is_self(k)))
+        def _():
+            col_copy(k).start()
+
+    @pl.when(to_self)
+    def _():
+        pcol[y] = mcol[...]
+
     copy_t = go(send(tv.at[theirs, :], tout_hbm.at[:, half], tout_sem, partner))
     store_t = pltpu.make_async_copy(tv.at[mine, :], tout_hbm.at[:, half], local_sem.at[4])
     store_t.start()
-    whole = part[y].astype(F32)
-    for j in range(1, NY):
-        frm = (y + NY - j) % NY
-        send(part.at[y], part.at[frm], part_sem.at[j], ypeer[j]).wait_recv()
-        whole = whole + part[frm].astype(F32)
-    norm = lax.rsqrt((whole[16:17] + whole[24:25]) * (1.0 / CH) + EPSILON)
-    sides = (whole[0:16] * norm).astype(BF16)
-    side[x] = sides
-    copy_side = go(send(side.at[x], side.at[x], side_sem.at[0], partner))
-    copy_c = send(side.at[x], side.at[2], side_sem.at[1], dest)
-
-    @pl.when(jnp.logical_not(to_self))
-    def _():
-        copy_c.start()
-
-    @pl.when(jnp.logical_not(to_self))
-    def _():
-        copy_c.wait_recv()
-
-    @pl.when(to_self)
-    def _():
-        side[2] = side[x]
-
-    copy_side.wait_recv()
-    sides_out[...] = side[...]
+    def finish(whole):
+        norm = lax.rsqrt((whole[8:9] + whole[12:13]) * (1.0 / CH) + EPSILON)
+        one = whole[0:8] * norm
+        return jnp.concatenate([one, one], axis=0).astype(BF16)
+
+    for column in range(2):
+        at = x if column == 0 else other
+        whole = None
+        for j in range(NY):
+            frm = (y + NY - j) % NY
+            if column == 1 or j > 0:
+                send(own, prow.at[at, frm], row_sem.at[column, j], partner).wait_recv()
+            term = prow[at, frm].astype(F32)
+            whole = term if whole is None else whole + term
+        side[at] = finish(whole)
+    whole = None
+    for k in range(NY):
+
+        @pl.when(jnp.logical_not(jnp.logical_and(to_self, y == k)))
+        def _():
+            pltpu.make_async_remote_copy(
+                src_ref=mcol, dst_ref=pcol.at[k], send_sem=col_out.at[k], recv_sem=col_in.at[k],
+                device_id=partner, device_id_type=MESH,
+            ).wait_recv()
+
+        term = pcol[k].astype(F32)
+        whole = term if whole is None else whole + term
+    side[2] = finish(whole)
+    store_s = pltpu.make_async_copy(side, sides_hbm, local_sem.at[9])
+    store_s.start()
 
     store_wide.wait()
     store_t.wait()
+    store_s.wait()
     send(tv.at[theirs, :], tout_hbm.at[:, other_half], tout_sem, partner).wait_recv()
     for copy in sent:
         copy.wait_send()
     edge_up.wait_send()
     edge_down.wait_send()
 
-    @pl.when(jnp.logical_not(to_self))
-    def _():
-        copy_c.wait_send()
+    for k in range(NY):
+
+        @pl.when(jnp.logical_not(col_is_self(k)))
+        def _():
+            col_copy(k).wait_send()
 
 
 def pair_kernel(
-    trunk_hbm, side, wide_hbm, pair_hbm, pb_hbm, tout_hbm, pout_hbm,
-    wide, pin, pov, pb, mix, rows_t, trunk, sem, in_sem, out_sem,
+    trunk_hbm, sides_hbm, wide_hbm, pair_hbm, pb_hbm, tout_hbm, pout_hbm,
+    side, wide, pin, pov, pb, mix, rows_t, trunk, sem, in_sem, out_sem,
 ):
     loads = [
         pltpu.make_async_copy(src, dst, sem.at[k])
-        for k, (src, dst) in enumerate(((wide_hbm, wide), (pb_hbm, pb)))
+        for k, (src, dst) in enumerate(((sides_hbm, side), (wide_hbm, wide), (pb_hbm, pb)))
     ]
     for copy in loads:
         copy.start()
@@ -440,19 +482,20 @@
     v_of = lax.broadcasted_iota(jnp.int32, (32, 256), 0)
     column = lax.broadcasted_iota(jnp.int32, (32, 256), 1)
     spread = jnp.where(column // 8 == v_of, 1.0, 0.0).astype(BF16)
-    s0 = side[0].astype(F32)
-    s1 = side[1].astype(F32)
-    cs = side[2].astype(F32)
-    low = lax.broadcasted_iota(jnp.int32, (16, 128), 1) < 32
+    loads[0].wait()
+    s0 = side[0].astype(F32)[0:8]
+    s1 = side[1].astype(F32)[0:8]
+    cs = side[2].astype(F32)[0:8]
+    low = lax.broadcasted_iota(jnp.int32, (8, 128), 1) < 32
+
+    def turned(block, by):
+        return block if by % 128 == 0 else pltpu.roll(block, by % 128, 1)
+
     row_t = jnp.concatenate(
-        [
-            jnp.where(low, s0, pltpu.roll(s1, 32, 1)),
-            jnp.where(low, pltpu.roll(s0, 96, 1), s1),
-        ],
-        axis=0,
+        [jnp.where(low, turned(s0, -32 * q), turned(s1, 32 - 32 * q)) for q in range(4)], axis=0
     )
     row_side = jnp.transpose(row_t)[0:64].astype(BF16)
-    col_t = jnp.concatenate([pltpu.roll(cs, 64, 1), pltpu.roll(cs, 32, 1)], axis=0)
+    col_t = jnp.concatenate([turned(cs, -32 * q) for q in range(4)], axis=0)
     col_side = jnp.transpose(col_t)[0:32].astype(BF16)
     repeated = jnp.dot(col_side, spread, preferred_element_type=F32)
     for i in range(8):
@@ -460,9 +503,9 @@
     load_t.wait()
     copy_t = pltpu.make_async_copy(trunk, tout_hbm, sem.at[4])
     copy_t.start()
-    loads[0].wait()
+    loads[1].wait()
     rows_t[...] = jnp.dot(row_side, wide[...], preferred_element_type=F32)
-    loads[1].wait()
+    loads[2].wait()
     for g in range(8):
         if g % 2 == 0:
             span = pl.ds(8 * g, 16)
@@ -496,7 +539,7 @@
             jax.ShapeDtypeStruct((32, 4096), BF16),
         ),
         in_specs=[hbm] * 6,
-        out_specs=(hbm, pl.BlockSpec(memory_space=pltpu.VMEM), hbm),
+        out_specs=(hbm, hbm, hbm),
         scratch_shapes=[
             pltpu.VMEM((OWN, 1024), BF16),
             pltpu.VMEM((TAPS, 2 * OWN, CH), BF16),
@@ -516,7 +559,9 @@
             pltpu.VMEM((2 * OWN, SEG), BF16),
             pltpu.VMEM((SEG, 128), BF16),
             pltpu.VMEM((64, 2 * OWN), BF16),
-            pltpu.VMEM((NY, 32, 128), BF16),
+            pltpu.VMEM((2, NY, 16, 128), BF16),
+            pltpu.VMEM((NY, 16, 128), BF16),
+            pltpu.VMEM((16, 128), BF16),
             pltpu.VMEM((3, 16, 128), BF16),
             pltpu.VMEM((1, OWN), F32),
             pltpu.VMEM((12, 128), F32),
@@ -535,8 +580,9 @@
             dma((2, 2)),
             dma((2,)),
             dma((2,)),
-            dma((NY, 2)),
-            dma((2, 2)),
+            dma((2, NY, 2)),
+            dma((NY,)),
+            dma((NY,)),
         ],
         compiler_params=pltpu.CompilerParams(
             collective_id=0, has_side_effects=True, vmem_limit_bytes=VMEM_LIMIT
@@ -555,9 +601,10 @@
             jax.ShapeDtypeStruct(trunk_in.shape, BF16),
             jax.ShapeDtypeStruct(pair_in.shape, BF16),
         ),
-        in_specs=[hbm, pl.BlockSpec(memory_space=pltpu.VMEM), hbm, hbm, hbm],
+        in_specs=[hbm] * 5,
         out_specs=(hbm, hbm),
         scratch_shapes=[
+            pltpu.VMEM((3, 16, 128), BF16),
             pltpu.VMEM((32, 4096), BF16),
             pltpu.VMEM((64, 32, 128), BF16),
             pltpu.VMEM((64, 32, 128), BF16),

time: 52.9 us -> 51.2 us (0.968)
  the two profiles are of different devices: /device:TPU:64 before, /device:TPU:1 now
where the time goes in v4:
time: 51.2 us; the launch traced here: 51 us
  Pallas kernels  50.4 us (98%)
  between operations  0.64 us (1%)
    pallas_call x1, Pallas kernels, per_device(): pl.pallas_call(kernel, name='trunk', out_shape=(jax.ShapeDtypeStruct(trun...  47.2 us
    pallas_call x1, Pallas kernels, per_device(): pl.pallas_call(pair_kernel, name='pair', out_shape=(jax.ShapeDtypeStruct(...  3.18 us

profile of v4, /device:TPU:1, one launch (start us, length us, event | category | flops | bytes accessed | tf_op | source)
XLA Modules:
  0.0 51.0 jit_solution(4786493747741013410)
XLA Ops:
  0.6 47.2 %trunk.1 = (bf16[96,1024]{1,0:T(8,128)(2,1)}, bf16[3,16,128]{2,1,0:T(8,128)(2,1)}, bf16[32,4096]{1,0:T(8,128)(2,1)}) custom-call(bf16[96,1024]{1,0:T(8,128)(2,1)} %x_hbm.1, bf16[5,96,1536]{2,1,0:T(8,128)(2,1)} %w_hbm.1, f32[1,96]{1,0:T(1,128)} %bitcast.5, f32[12,128]{1,0:T(8,128)} %bitcast.4, bf16[64,1536]{1,0:T(8,128)(2,1)} %pp_hbm.1, bf16[1024,128]{1,0:T(8,128)(2,1)} %opm_hbm.1), custom_call_target="tpu_custom_call" | custom-call | flops 1600000000 | bytes 3000000 | tf_op jit(solution)/shard_map/trunk/pallas_call | solution.py:533
  47.8 3.2 %pair.1 = (bf16[96,1024]{1,0:T(8,128)(2,1)}, bf16[64,32,128]{2,1,0:T(8,128)(2,1)}) custom-call(bf16[96,1024]{1,0:T(8,128)(2,1)} %get-tuple-element.5.trunk_hbm, bf16[3,16,128]{2,1,0:T(8,128)(2,1)} %get-tuple-element.6.sides_hbm, bf16[32,4096]{1,0:T(8,128)(2,1)} %get-tuple-element.7.wide_hbm, bf16[64,32,128]{2,1,0:T(8,128)(2,1)} %pair_hbm.1, f32[1,128]{1,0:T(1,128)} %bitcast.3), custom_call_target="tpu_custom_call" | custom-call | flops 200000000 | bytes 2000000 | tf_op jit(solution)/shard_map/pair/pallas_call | solution.py:597

commit v5 on v4

--- a/solution.py
+++ b/solution.py
@@ -327,21 +327,17 @@
     load_w.wait()
     send(wbuf.at[:, theirs, k_rest], wbuf.at[:, theirs, k_rest], sib_sem, sibling).wait_recv()
 
-    def product(tap, group):
+    def product(group):
         out = None
         for k in range(2):
             span = pl.ds(pl.multiple_of(768 * k + 384 * group, 128), 384)
-            term = jnp.dot(wbuf[tap, :, span], act[span, :], preferred_element_type=F32)
+            weights = wbuf[:, :, span].reshape(TAPS * 2 * OWN, 384)
+            term = jnp.dot(weights, act[span, :], preferred_element_type=F32)
             out = term if out is None else out + term
-        return out
+        return out.reshape(TAPS, 2 * OWN, EXT)
 
     group = y // 4
-
-    def early(tap, carry):
-        taps[tap] = product(tap, group)
-        return carry
-
-    lax.fori_loop(0, TAPS, early, 0)
+    taps[...] = product(group)
 
     for piece in range(2):
         step(0, 4, piece)
@@ -352,8 +348,9 @@
         step(1, 4, piece)
     activate(1, ahead(4))
 
+    late = product(1 - group)
     for tap in range(TAPS):
-        full = taps[tap] + product(tap, 1 - group)
+        full = taps[tap] + late[tap]
         delta = STEP * (tap - 2)
         if delta != 0:
             full = pltpu.roll(full, (-delta) % EXT, 1)

time: 51.2 us -> 51.2 us (level)
  no operation moved by 1% of the time
where the time goes in v5:
time: 51.2 us; the launch traced here: 51 us
  Pallas kernels  50.4 us (98%)
  between operations  0.64 us (1%)
    pallas_call x1, Pallas kernels, per_device(): pl.pallas_call(kernel, name='trunk', out_shape=(jax.ShapeDtypeStruct(trun...  47.2 us
    pallas_call x1, Pallas kernels, per_device(): pl.pallas_call(pair_kernel, name='pair', out_shape=(jax.ShapeDtypeStruct(...  3.2 us

profile of v5, /device:TPU:1, one launch (start us, length us, event | category | flops | bytes accessed | tf_op | source)
XLA Modules:
  0.0 51.0 jit_solution(13553715963401730136)
XLA Ops:
  0.6 47.2 %trunk.1 = (bf16[96,1024]{1,0:T(8,128)(2,1)}, bf16[3,16,128]{2,1,0:T(8,128)(2,1)}, bf16[32,4096]{1,0:T(8,128)(2,1)}) custom-call(bf16[96,1024]{1,0:T(8,128)(2,1)} %x_hbm.1, bf16[5,96,1536]{2,1,0:T(8,128)(2,1)} %w_hbm.1, f32[1,96]{1,0:T(1,128)} %bitcast.5, f32[12,128]{1,0:T(8,128)} %bitcast.4, bf16[64,1536]{1,0:T(8,128)(2,1)} %pp_hbm.1, bf16[1024,128]{1,0:T(8,128)(2,1)} %opm_hbm.1), custom_call_target="tpu_custom_call" | custom-call | flops 1600000000 | bytes 3000000 | tf_op jit(solution)/shard_map/trunk/pallas_call | solution.py:530
  47.8 3.2 %pair.1 = (bf16[96,1024]{1,0:T(8,128)(2,1)}, bf16[64,32,128]{2,1,0:T(8,128)(2,1)}) custom-call(bf16[96,1024]{1,0:T(8,128)(2,1)} %get-tuple-element.5.trunk_hbm, bf16[3,16,128]{2,1,0:T(8,128)(2,1)} %get-tuple-element.6.sides_hbm, bf16[32,4096]{1,0:T(8,128)(2,1)} %get-tuple-element.7.wide_hbm, bf16[64,32,128]{2,1,0:T(8,128)(2,1)} %pair_hbm.1, f32[1,128]{1,0:T(1,128)} %bitcast.3), custom_call_target="tpu_custom_call" | custom-call | flops 200000000 | bytes 2000000 | tf_op jit(solution)/shard_map/pair/pallas_call | solution.py:594
